TPU v7x, 32 devices: a whole 2x2x4 slice. The times are simulated.
32 devices in a mesh: seq: 8 (over z, core), tp: 4 (over y, x).
Axes of the slice: x: 2, y: 2, z: 4, core: 2. Of those that a mesh axis runs over, the one named last changes fastest.
Arguments:
- tokens: bfloat16 [2, 1536, 4096], P(None, 'seq', 'tp'), may hold values from -6 to 6
- gate_weight: bfloat16 [4096, 4096], P(None, 'tp'), may hold values from -0.09375 to 0.09375
- cand_weight: bfloat16 [4096, 4096], P(None, 'tp'), may hold values from -0.09375 to 0.09375
- forget_bias: float32 [4096], P('tp'), may hold values from -1 to 9
- readout: bfloat16 [2, 1536, 4096], P(None, 'seq', 'tp'), may hold values from -6 to 6
- advantage: int32 [2, 1536], P(None, 'seq'), may hold values from -4 to 4
Outputs:
- grad_gate: float32 [4096, 4096], P('seq', 'tp')
- grad_cand: float32 [4096, 4096], P('seq', 'tp')
- grad_tokens: bfloat16 [2, 1536, 4096], P(None, 'seq', 'tp')
All inputs are finite; a program needn't handle non-finite values.
Results may differ from a plain program's by a relative error of at most 0.014.
Values may be sent and summed in bfloat16 or wider, within the bound.
A program may use at most 128 MiB of HBM per device.

v0:
```python
import jax
import jax.numpy as jnp
from jax import lax
from jax.sharding import PartitionSpec as P


def from_behind(block, axis, distance):
    devices = range(lax.axis_size(axis))
    route = [(i - distance, i) for i in devices if i - distance in devices]
    return lax.ppermute(block, axis, route)


def compose(earlier, later):
    return (earlier[0] * later[0], later[0] * earlier[1] + later[1])


def shards(tokens, gate_weight, cand_weight, forget_bias, readout, advantage):
    whole = lax.all_gather(tokens, "tp", axis=2, tiled=True)
    count = whole.shape[1]
    width = gate_weight.shape[1]
    flat = whole.reshape(-1, whole.shape[2])
    pre = jnp.dot(flat, gate_weight, preferred_element_type=jnp.float32).reshape(2, count, width)
    cand = jnp.dot(flat, cand_weight, preferred_element_type=jnp.float32).reshape(2, count, width)
    keep = jax.nn.sigmoid(pre + forget_bias)
    prod_keep, local_state = lax.associative_scan(compose, (keep, (1.0 - keep) * cand), axis=1)
    span_mul = prod_keep[:, -1]
    span_add = local_state[:, -1]
    devices = lax.axis_size("seq")

    def forward_link(step, incoming):
        return from_behind(span_mul * incoming + span_add, "seq", 1)

    state_in = lax.fori_loop(0, devices - 1, forward_link, jnp.zeros_like(span_add))
    state = local_state + prod_keep * state_in[:, None]
    prev = jnp.concatenate([state_in[:, None], state[:, :-1]], axis=1)
    score = (advantage.astype(jnp.float32) * 0.25)[:, :, None] * readout.astype(jnp.float32)
    coef = jnp.concatenate([keep[:, 1:], jnp.ones_like(keep[:, :1])], axis=1)
    reach, local_adj = lax.associative_scan(compose, (coef, score), reverse=True, axis=1)
    back_mul = keep[:, 0] * reach[:, 0]
    back_add = keep[:, 0] * local_adj[:, 0]

    def backward_link(step, incoming):
        return from_behind(back_mul * incoming + back_add, "seq", -1)

    adjoint_in = lax.fori_loop(0, devices - 1, backward_link, jnp.zeros_like(back_add))
    adjoint = local_adj + reach * adjoint_in[:, None]
    dpre = (adjoint * (prev - cand) * keep * (1.0 - keep)).astype(jnp.bfloat16).reshape(-1, width)
    dcand = (adjoint * (1.0 - keep)).astype(jnp.bfloat16).reshape(-1, width)
    deltas = jnp.concatenate([dpre, dcand], axis=1)
    column_part = lax.all_to_all(flat, "seq", split_axis=1, concat_axis=0, tiled=True)
    both = lax.dot_general(
        column_part,
        lax.all_gather(deltas, "seq", axis=0, tiled=True),
        (((0,), (0,)), ((), ())),
        preferred_element_type=jnp.float32,
    )
    grad_gate = both[:, :width]
    grad_cand = both[:, width:]
    contract = (((1,), (1,)), ((), ()))
    term = lax.dot_general(dpre, gate_weight, contract, preferred_element_type=jnp.float32)
    term = term + lax.dot_general(dcand, cand_weight, contract, preferred_element_type=jnp.float32)
    term = term.reshape(2, count, flat.shape[1])
    grad_tokens = lax.psum_scatter(term, "tp", scatter_dimension=2, tiled=True).astype(jnp.bfloat16)
    return (grad_gate, grad_cand, grad_tokens)


def solution(mesh):
    in_specs = (
        P(None, "seq", "tp"),
        P(None, "tp"),
        P(None, "tp"),
        P("tp"),
        P(None, "seq", "tp"),
        P(None, "seq"),
    )
    out_specs = (P("seq", "tp"), P("seq", "tp"), P(None, "seq", "tp"))
    return jax.shard_map(shards, mesh=mesh, in_specs=in_specs, out_specs=out_specs, check_vma=False)
```

profile of v0, /device:TPU:0, one launch (start us, length us, event | category | flops | bytes accessed | tf_op | source)
XLA Modules:
  0.0 671.4 jit_solution(7339538003626025138)
XLA Ops:
  13.5 8.6 %slice.465 = f32[2,96,1024]{2,1,0:T(8,128)} reverse(f32[2,96,1024]{2,1,0:T(8,128)} %slice.464), dimensions={1} | reverse | bytes 1572864 | tf_op jit(solution)/shard_map/slice | solution.py:38
  22.1 5.2 slice.467
  27.3 5.2 slice.517
  32.5 24.0 %all-gather.3.cloned.1.call-done = bf16[2,192,4096]{2,1,0:T(8,128)(2,1)} async-done(((bf16[2,192,1024]{2,1,0:T(8,128)(2,1)}), bf16[2,192,4096]{2,1,0:T(8,128)(2,1)}) %all-gather.3.cloned.1.call-update) | async-done | bytes 3145744 | tf_op jit(solution)/shard_map/all_gather | solution.py:18
  56.6 7.0 %add_divide_fusion = f32[2,192,1024]{2,1,0:T(8,128)S(1)} fusion(bf16[2,192,4096]{2,1,0:T(8,128)(2,1)} %all-gather.3.cloned.1.call-done, bf16[4096,1024]{1,0:T(8,128)(2,1)} %param.11, f32[1024]{0:T(1024)S(1)} %copy-done.62), kind=kOutput, calls=%fused_computation.17 | convolution fusion | flops 3222798336 | bytes 13111296 | tf_op jit(solution)/shard_map/dot_general | solution.py:22
  68.3 8.5 %slice.463 = f32[2,96,1024]{2,1,0:T(8,128)} reverse(f32[2,96,1024]{2,1,0:T(8,128)} %slice.462), dimensions={1} | reverse | bytes 1572864 | tf_op jit(solution)/shard_map/slice | solution.py:38
  76.9 8.5 %slice.470 = f32[2,96,1024]{2,1,0:T(8,128)} reverse(f32[2,96,1024]{2,1,0:T(8,128)} %slice.469), dimensions={1} | reverse | bytes 1572864 | tf_op jit(solution)/shard_map/slice | solution.py:38
  85.4 3.4 fusion.33
  156.9 8.7 %slice.461 = f32[2,95,1024]{2,1,0:T(8,128)} reverse(f32[2,95,1024]{2,1,0:T(8,128)} %slice.460), dimensions={1} | reverse | bytes 1556480 | tf_op jit(solution)/shard_map/slice | solution.py:38
  177.4 2.7 pad.199
  193.1 3.4 pad.186
  196.6 3.4 pad.200
  199.9 3.4 pad.201
  203.3 3.5 add.348
  210.8 8.0 %subtract_multiply_fusion = (f32[2,192,1024]{2,1,0:T(8,128)S(1)}, f32[2,192,1024]{2,1,0:T(8,128)}) fusion(f32[2,192,1024]{2,1,0:T(8,128)S(1)} %add_divide_fusion, bf16[2,192,4096]{2,1,0:T(8,128)(2,1)S(1)} %copy-done.10, bf16[4096,1024]{1,0:T(8,128)(2,1)} %param.12), kind=kOutput, calls=%fused_computation.19 | convolution fusion | flops 3222011904 | bytes 16252928 | tf_op jit(solution)/shard_map/dot_general | solution.py:23
  288.5 4.5 slice.598
  297.4 10.4 %rev.9 = f32[2,192,1024]{2,1,0:T(8,128)} reverse(f32[2,192,1024]{2,1,0:T(8,128)S(1)} %copy-done.6), dimensions={1} | reverse | bytes 3145728 | tf_op jit(solution)/shard_map/rev | solution.py:38
  307.9 16.2 %rev.8 = f32[2,192,1024]{2,1,0:T(8,128)} reverse(f32[2,192,1024]{2,1,0:T(8,128)} %add.341), dimensions={1} | reverse | bytes 3145728 | tf_op jit(solution)/shard_map/rev | solution.py:38
  338.9 3.4 pad.378
  343.8 2.7 pad.212
  361.4 3.4 pad.379
  370.7 31.9 %while.21 = (s32[]{:T(128)}, f32[2,1024]{1,0:T(2,128)S(1)}, f32[2,1024]{1,0:T(2,128)S(1)}, f32[2,1024]{1,0:T(2,128)S(1)}, s32[]{:T(128)}) while((s32[]{:T(128)}, f32[2,1024]{1,0:T(2,128)S(1)}, f32[2,1024]{1,0:T(2,128)S(1)}, f32[2,1024]{1,0:T(2,128)S(1)}, s32[]{:T(128)}) %tuple.97), condition=%wide.region_3.0_spmd, body=%wide.region_2.0_spmd.sunk | while | flops 4098 | bytes 65637 | solution.py:33
  373.2 3.6 collective-permute-start.1
  377.7 4.2 collective-permute-start.1
  382.7 4.2 collective-permute-start.1
  387.7 4.2 collective-permute-start.1
  392.6 4.2 collective-permute-start.1
  397.6 4.2 collective-permute-start.1
  402.6 4.9 multiply_add_fusion.2
  407.6 35.3 %while.20 = (s32[]{:T(128)}, f32[2,1024]{1,0:T(2,128)S(1)}, f32[2,1024]{1,0:T(2,128)S(1)}, f32[2,1024]{1,0:T(2,128)S(1)}, s32[]{:T(128)}) while((s32[]{:T(128)}, f32[2,1024]{1,0:T(2,128)S(1)}, f32[2,1024]{1,0:T(2,128)S(1)}, f32[2,1024]{1,0:T(2,128)S(1)}, s32[]{:T(128)}) %tuple.95), condition=%wide.region_1.0_spmd, body=%wide.region_0.0_spmd.sunk | while | flops 4098 | bytes 65637 | solution.py:45
  408.9 3.5 collective-permute-done
  413.7 4.2 collective-permute-done
  419.2 3.7 collective-permute-done
  424.2 3.7 collective-permute-done
  429.2 3.7 collective-permute-done
  434.2 3.7 collective-permute-done
  439.2 3.7 collective-permute-done
  442.8 3.5 fusion.7
  446.4 6.5 fusion.44
  452.9 5.3 convolution_add_fusion
  458.6 2.8 pad_maximum_fusion
  462.8 2.7 copy.11
  465.6 5.7 all-to-all-start
  471.3 58.5 %reduce-scatter.2.cloned.1.call-done = f32[2,192,1024]{2,1,0:T(8,128)} async-done(((f32[2,192,4096]{2,1,0:T(8,128)}), f32[2,192,1024]{2,1,0:T(8,128)}) %reduce-scatter.2.cloned.1.call-update) | async-done | bytes 1572880 | tf_op jit(solution)/shard_map/reduce_scatter | solution.py:63
  532.2 10.6 %all-to-all-done = bf16[384,8,512]{2,0,1:T(8,128)(2,1)S(1)} async-done(((bf16[384,8,512]{2,0,1:T(8,128)(2,1)}), bf16[384,8,512]{2,0,1:T(8,128)(2,1)S(1)}, u32[]{:S(2)}, u32[]{:S(2)}) %all-to-all-start) | async-done | bytes 3145760 | tf_op jit(solution)/shard_map/all_to_all | solution.py:50
  542.8 105.9 %all-gather.5.cloned.1.call-done = bf16[3072,2048]{1,0:T(8,128)(2,1)} async-done(((bf16[384,2048]{1,0:T(8,128)(2,1)}), bf16[3072,2048]{1,0:T(8,128)(2,1)}) %all-gather.5.cloned.1.call-update) | async-done | bytes 12582928 | tf_op jit(solution)/shard_map/all_gather | solution.py:53
  648.8 9.7 %convolution_bitcast_fusion = f32[512,2048]{0,1:T(8,128)S(1)} fusion(bf16[3072,2048]{1,0:T(8,128)(2,1)} %all-gather.5.cloned.1.call-done, bf16[3072,512]{1,0:T(8,128)(2,1)S(1)} %bitcast.44), kind=kOutput, calls=%fused_computation.7 | convolution fusion | flops 6442450944 | bytes 19922944 | tf_op jit(solution)/shard_map/dot_general | solution.py:51
  660.2 2.9 copy.12
  (398 shorter events, 242.3 us)
Async XLA Ops:
  7.2 49.4 %all-gather.3.cloned.1.call-start = ((), (), s32[]{:S(2)}) async-start(), calls=%async_computation.2 | async-start | bytes 3932160 | tf_op jit(solution)/shard_map/all_gather | solution.py:18
  7.9 521.9 %reduce-scatter.2.cloned.1.call-start = ((), (), s32[]{:S(2)}) async-start(), calls=%async_computation.4 | async-start | bytes 7864320 | tf_op jit(solution)/shard_map/reduce_scatter | solution.py:63
  22.1 34.4 %copy-start.62 = (f32[1024]{0:T(1024)S(1)}, f32[1024]{0:T(1024)}, u32[]{:S(2)}) copy-start(f32[1024]{0:T(1024)} %param.13) | copy-start | bytes 12292
  156.8 8.8 %copy-start.36 = (f32[2,3,1024]{2,1,0:T(4,128)S(1)}, f32[2,3,1024]{2,1,0:T(4,128)}, u32[]{:S(2)}) copy-start(f32[2,3,1024]{2,1,0:T(4,128)} %slice.497) | copy-start | bytes 73732
  156.8 8.8 %copy-start.37 = (f32[2,3,1024]{2,1,0:T(4,128)S(1)}, f32[2,3,1024]{2,1,0:T(4,128)}, u32[]{:S(2)}) copy-start(f32[2,3,1024]{2,1,0:T(4,128)} %slice.498) | copy-start | bytes 73732
  156.8 8.8 %copy-start.38 = (f32[2,3,1024]{2,1,0:T(4,128)S(1)}, f32[2,3,1024]{2,1,0:T(4,128)}, u32[]{:S(2)}) copy-start(f32[2,3,1024]{2,1,0:T(4,128)} %slice.496) | copy-start | bytes 73732
  156.8 8.8 %copy-start.39 = (f32[2,3,1024]{2,1,0:T(4,128)S(1)}, f32[2,3,1024]{2,1,0:T(4,128)}, u32[]{:S(2)}) copy-start(f32[2,3,1024]{2,1,0:T(4,128)} %slice.500) | copy-start | bytes 73732
  156.8 9.1 %copy-start.42 = (f32[2,2,1024]{2,1,0:T(2,128)S(1)}, f32[2,2,1024]{2,1,0:T(2,128)}, u32[]{:S(2)}) copy-start(f32[2,2,1024]{2,1,0:T(2,128)} %slice.506) | copy-start | bytes 49156
  156.8 9.2 %copy-start.51 = (f32[2,1,1024]{2,1,0:T(1,128)S(1)}, f32[2,1,1024]{2,1,0:T(1,128)}, u32[]{:S(2)}) copy-start(f32[2,1,1024]{2,1,0:T(1,128)} %slice.609) | copy-start | bytes 24580
  156.8 9.2 %copy-start.52 = (f32[2,1,1024]{2,1,0:T(1,128)S(1)}, f32[2,1,1024]{2,1,0:T(1,128)}, u32[]{:S(2)}) copy-start(f32[2,1,1024]{2,1,0:T(1,128)} %slice.631) | copy-start | bytes 24580
  156.8 9.3 %copy-start.30 = (f32[2,5,1024]{2,1,0:T(8,128)S(1)}, f32[2,5,1024]{2,1,0:T(8,128)}, u32[]{:S(2)}) copy-start(f32[2,5,1024]{2,1,0:T(8,128)} %slice.489) | copy-start | bytes 122884
  156.9 9.3 %copy-start.31 = (f32[2,5,1024]{2,1,0:T(8,128)S(1)}, f32[2,5,1024]{2,1,0:T(8,128)}, u32[]{:S(2)}) copy-start(f32[2,5,1024]{2,1,0:T(8,128)} %slice.508) | copy-start | bytes 122884
  156.9 9.4 %copy-start.61 = (f32[2,1,1024]{2,1,0:T(1,128)S(1)}, f32[2,1,1024]{2,1,0:T(1,128)}, u32[]{:S(2)}) copy-start(f32[2,1,1024]{2,1,0:T(1,128)} %slice.608) | copy-start | bytes 24580
  176.4 3.7 copy-start.16
  176.4 3.7 copy-start.45
  203.3 3.5 copy-start.4
  218.8 4.4 copy-start.7
  288.5 8.9 %copy-start.6 = (f32[2,192,1024]{2,1,0:T(8,128)S(1)}, f32[2,192,1024]{2,1,0:T(8,128)}, u32[]{:S(2)}) copy-start(f32[2,192,1024]{2,1,0:T(8,128)} %add.348) | copy-start | bytes 4718596
  307.8 16.2 %copy-start.32 = (f32[2,3,1024]{2,1,0:T(4,128)S(1)}, f32[2,3,1024]{2,1,0:T(4,128)}, u32[]{:S(2)}) copy-start(f32[2,3,1024]{2,1,0:T(4,128)} %slice.548) | copy-start | bytes 73732
  307.8 16.2 %copy-start.33 = (f32[2,3,1024]{2,1,0:T(4,128)S(1)}, f32[2,3,1024]{2,1,0:T(4,128)}, u32[]{:S(2)}) copy-start(f32[2,3,1024]{2,1,0:T(4,128)} %slice.549) | copy-start | bytes 73732
  307.8 16.2 %copy-start.34 = (f32[2,3,1024]{2,1,0:T(4,128)S(1)}, f32[2,3,1024]{2,1,0:T(4,128)}, u32[]{:S(2)}) copy-start(f32[2,3,1024]{2,1,0:T(4,128)} %slice.582) | copy-start | bytes 73732
  307.8 16.2 %copy-start.35 = (f32[2,3,1024]{2,1,0:T(4,128)S(1)}, f32[2,3,1024]{2,1,0:T(4,128)}, u32[]{:S(2)}) copy-start(f32[2,3,1024]{2,1,0:T(4,128)} %slice.583) | copy-start | bytes 73732
  307.8 16.5 %copy-start.40 = (f32[2,2,1024]{2,1,0:T(2,128)S(1)}, f32[2,2,1024]{2,1,0:T(2,128)}, u32[]{:S(2)}) copy-start(f32[2,2,1024]{2,1,0:T(2,128)} %slice.554) | copy-start | bytes 49156
  307.8 16.5 %copy-start.41 = (f32[2,2,1024]{2,1,0:T(2,128)S(1)}, f32[2,2,1024]{2,1,0:T(2,128)}, u32[]{:S(2)}) copy-start(f32[2,2,1024]{2,1,0:T(2,128)} %slice.588) | copy-start | bytes 49156
  307.9 16.6 %copy-start.49 = (f32[2,1,1024]{2,1,0:T(1,128)S(1)}, f32[2,1,1024]{2,1,0:T(1,128)}, u32[]{:S(2)}) copy-start(f32[2,1,1024]{2,1,0:T(1,128)} %slice.654) | copy-start | bytes 24580
  307.9 16.6 %copy-start.50 = (f32[2,1,1024]{2,1,0:T(1,128)S(1)}, f32[2,1,1024]{2,1,0:T(1,128)}, u32[]{:S(2)}) copy-start(f32[2,1,1024]{2,1,0:T(1,128)} %slice.677) | copy-start | bytes 24580
  338.9 3.4 copy-start.17
  370.7 2.6 collective-permute-start.1
  373.2 4.4 collective-permute-start.1
  377.7 5.0 collective-permute-start.1
  382.7 5.0 collective-permute-start.1
  387.7 5.0 collective-permute-start.1
  392.6 5.0 collective-permute-start.1
  397.6 5.0 collective-permute-start.1
  402.6 40.2 %copy-start.5 = (f32[2,192,1024]{2,1,0:T(8,128)S(1)}, f32[2,192,1024]{2,1,0:T(8,128)}, u32[]{:S(2)}) copy-start(f32[2,192,1024]{2,1,0:T(8,128)} %rev.9) | copy-start | bytes 4718596
  407.6 4.8 collective-permute-start
  412.4 5.5 collective-permute-start
  417.9 5.0 collective-permute-start
  422.9 5.0 collective-permute-start
  427.9 5.0 collective-permute-start
  432.9 5.0 collective-permute-start
  437.9 5.0 collective-permute-start
  442.8 10.1 %slice-start = ((s8[8388608]{0:T(1024)(128)(4,1)}), s8[4194304]{0:T(1024)(128)(4,1)S(1)}, s32[]{:S(2)}) async-start(s8[8388608]{0:T(1024)(128)(4,1)} %bitcast.53), calls=%async_computation.5 | async-start | bytes 8388608
  446.4 6.5 copy-start.12
  446.4 6.5 copy-start.13
  446.4 6.5 slice-start.1
  458.3 190.5 %all-gather.5.cloned.1.call-start = ((), (), s32[]{:S(2)}) async-start(), calls=%async_computation.3 | async-start | bytes 14155776 | tf_op jit(solution)/shard_map/all_gather | solution.py:53
  465.6 77.2 %all-to-all-start = ((bf16[384,8,512]{2,0,1:T(8,128)(2,1)}), bf16[384,8,512]{2,0,1:T(8,128)(2,1)S(1)}, u32[]{:S(2)}, u32[]{:S(2)}) async-start(bf16[384,8,512]{2,0,1:T(8,128)(2,1)} %copy.11), calls=%async_computation | async-start | bytes 6291456 | tf_op jit(solution)/shard_map/all_to_all | solution.py:50
  (35 other events, 62.4 us)
Sparse Core Ops, SparseCore 0:
  9.8 46.6 all-gather.2
  458.4 71.3 reduce-scatter.1
  532.0 116.7 all-gather.4
where the time goes:
time: 680 us; the launch traced here: 671 us
  local copies, waits for them, and re-layouts  270 us (40%)
  waiting for transfers between devices  232 us (34%)
  other arithmetic  76.9 us (11%)
  starting transfers between devices  41.2 us (6%)
  matrix products  36.5 us (5%)
  between operations  15 us (2%)
    slice x53, local copies, waits for them, and re-layouts, shards(): lax.associative_scan(compose, (coef, score), reverse=True, axis=1)  113 us
    all_gather x1, waiting for transfers between devices, shards(): lax.all_gather(deltas, 'seq', axis=0, tiled=True)  106 us
    slice x47, local copies, waits for them, and re-layouts, shards(): lax.associative_scan(compose, (keep, (1.0 - keep) * cand), axis=1)  68.1 us
    reduce_scatter x1, waiting for transfers between devices, shards(): lax.psum_scatter(term, 'tp', scatter_dimension=2, tiled=True)  58.5 us
    ppermute x14, starting transfers between devices, from_behind(): return lax.ppermute(block, axis, route)  35.2 us
    ppermute x14, waiting for transfers between devices, from_behind(): return lax.ppermute(block, axis, route)  31.7 us
    mul x26, other arithmetic, compose(): return (earlier[0] * later[0], later[0] * earlier[1] + later[1])  29.5 us
    rev x2, local copies, waits for them, and re-layouts, shards(): lax.associative_scan(compose, (coef, score), reverse=True, axis=1)  26.6 us
  transfers between devices with their start and end apart: 18, of which 18 were waited for; matrix products, arithmetic and copies ran while one was open for 5% of the time, Pallas kernels for 0%

commit v1 on v0

v1 whole, which is shorter than its diff:
```python
import functools

import jax
import jax.numpy as jnp
from jax import lax
from jax.experimental import pallas as pl
from jax.experimental.pallas import tpu as pltpu
from jax.sharding import PartitionSpec as P

SEGS = 8
LANE = 128


def project_kernel(flat, gate, cand_w, bias, read, scale, keep_out, cand_out, seg_out, span_out, score):
    count = flat.shape[0] // 2
    steps = count // SEGS
    lanes = gate.shape[1] // LANE
    pre = jnp.dot(flat[...], gate[...], preferred_element_type=jnp.float32)
    keep = jax.nn.sigmoid(pre + bias[...])
    cand = jnp.dot(flat[...], cand_w[...], preferred_element_type=jnp.float32)
    value = scale[...] * read[...].astype(jnp.float32)
    for l in range(lanes):
        keep_out[l] = keep[:, l * LANE : (l + 1) * LANE]
        cand_out[l] = cand[:, l * LANE : (l + 1) * LANE]
        score[l] = value[:, l * LANE : (l + 1) * LANE]
    span_out[...] = jnp.zeros_like(span_out)
    zero = jnp.zeros((SEGS, LANE), jnp.float32)
    pairs = [(b, l) for b in range(2) for l in range(lanes)]
    muls = [zero + 1.0 for _ in pairs]
    adds = [zero for _ in pairs]
    gs = [zero for _ in pairs]
    for i in range(steps):
        for p, (b, l) in enumerate(pairs):
            rows = pl.ds(b * count + i, SEGS, stride=steps)
            k = keep_out[l, rows, :]
            c = cand_out[l, rows, :]
            muls[p] = muls[p] * k
            adds[p] = k * adds[p] + (1.0 - k) * c
            rows = pl.ds(b * count + steps - 1 - i, SEGS, stride=steps)
            gs[p] = keep_out[l, rows, :] * (score[l, rows, :] + gs[p])
    for p, (b, l) in enumerate(pairs):
        at = slice(l * LANE, (l + 1) * LANE)
        mul, add, g = muls[p], adds[p], gs[p]
        seg_out[0, b, :, at] = mul
        seg_out[1, b, :, at] = add
        seg_out[2, b, :, at] = g
        m = mul[0:1]
        a = add[0:1]
        r = g[SEGS - 1 :]
        for j in range(1, SEGS):
            m = m * mul[j : j + 1]
            a = mul[j : j + 1] * a + add[j : j + 1]
            e = SEGS - 1 - j
            r = mul[e : e + 1] * r + g[e : e + 1]
        span_out[b : b + 1, at] = m
        span_out[2 + b : 3 + b, at] = a
        span_out[4 + b : 5 + b, at] = r


def delta_kernel(devices, where, spans, seg, keep, cand, read, scale, dpre_out, dcand_out, score, dp, dc):
    lanes, rows_all, _ = keep.shape
    count = rows_all // 2
    steps = count // SEGS
    me = where[0]
    value = scale[...] * read[...].astype(jnp.float32)
    pairs = [(b, l) for b in range(2) for l in range(lanes)]
    states, tails = [], []
    for l in range(lanes):
        score[l] = value[:, l * LANE : (l + 1) * LANE]
    for b, l in pairs:
        at = slice(l * LANE, (l + 1) * LANE)
        a = jnp.zeros((1, LANE), jnp.float32)
        r = a
        for d in range(devices):
            e = devices - 1 - d
            a = jnp.where(d < me, spans[d, b : b + 1, at] * a + spans[d, 2 + b : 3 + b, at], a)
            r = jnp.where(e > me, spans[e, b : b + 1, at] * r + spans[e, 4 + b : 5 + b, at], r)
        mul, add, g = seg[0, b, :, at], seg[1, b, :, at], seg[2, b, :, at]
        starts, ends = [a], [r]
        for j in range(SEGS - 1):
            a = mul[j : j + 1] * a + add[j : j + 1]
            starts.append(a)
            e = SEGS - 1 - j
            r = mul[e : e + 1] * r + g[e : e + 1]
            ends.append(r)
        states.append(jnp.concatenate(starts, axis=0))
        tails.append(jnp.concatenate(ends[::-1], axis=0))
    for i in range(steps):
        for p, (b, l) in enumerate(pairs):
            rows = pl.ds(b * count + i, SEGS, stride=steps)
            k = keep[l, rows, :]
            c = cand[l, rows, :]
            dp[l, rows, :] = (states[p] - c) * k * (1.0 - k)
            states[p] = k * states[p] + (1.0 - k) * c
    for i in range(steps):
        for p, (b, l) in enumerate(pairs):
            rows = pl.ds(b * count + steps - 1 - i, SEGS, stride=steps)
            k = keep[l, rows, :]
            adj = score[l, rows, :] + tails[p]
            dp[l, rows, :] = adj * dp[l, rows, :]
            dc[l, rows, :] = adj * (1.0 - k)
            tails[p] = k * adj
    for l in range(lanes):
        at = slice(l * LANE, (l + 1) * LANE)
        dpre_out[:, at] = dp[l].astype(jnp.bfloat16)
        dcand_out[:, at] = dc[l].astype(jnp.bfloat16)


def shards(tokens, gate_weight, cand_weight, forget_bias, readout, advantage):
    devices = lax.axis_size("seq")
    groups = lax.axis_size("tp")
    whole = lax.all_gather(tokens, "tp", axis=2, tiled=True)
    count = whole.shape[1]
    depth = whole.shape[2]
    rows = 2 * count
    width = gate_weight.shape[1]
    flat = whole.reshape(rows, depth)
    part = rows // groups
    mine = lax.dynamic_slice_in_dim(flat, lax.axis_index("tp") * part, part, 0)
    mine = lax.all_to_all(mine, "seq", split_axis=1, concat_axis=0, tiled=True)
    cols = lax.all_gather(mine, "tp", axis=0, tiled=False)
    cols = cols.reshape(groups, devices, part, depth // devices)
    cols = jnp.transpose(cols, (1, 0, 2, 3)).reshape(devices * rows, depth // devices)

    scale = (advantage.astype(jnp.float32) * 0.25).reshape(rows, 1)
    read = readout.reshape(rows, width)
    tile = 256 if width % 256 == 0 else width
    f32 = jnp.float32
    col = pl.BlockSpec((rows, tile), lambda i: (0, i))
    lane = pl.BlockSpec((tile // LANE, rows, LANE), lambda i: (i, 0, 0))
    full_scale = pl.BlockSpec((rows, 1), lambda i: (0, 0))
    seg_spec = pl.BlockSpec((3, 2, SEGS, tile), lambda i: (0, 0, 0, i))
    keep, cand, seg, span = pl.pallas_call(
        project_kernel,
        grid=(width // tile,),
        in_specs=[
            pl.BlockSpec((rows, depth), lambda i: (0, 0)),
            pl.BlockSpec((depth, tile), lambda i: (0, i)),
            pl.BlockSpec((depth, tile), lambda i: (0, i)),
            pl.BlockSpec((1, tile), lambda i: (0, i)),
            col,
            full_scale,
        ],
        out_specs=[lane, lane, seg_spec, pl.BlockSpec((8, tile), lambda i: (0, i))],
        out_shape=[
            jax.ShapeDtypeStruct((width // LANE, rows, LANE), f32),
            jax.ShapeDtypeStruct((width // LANE, rows, LANE), f32),
            jax.ShapeDtypeStruct((3, 2, SEGS, width), f32),
            jax.ShapeDtypeStruct((8, width), f32),
        ],
        scratch_shapes=[pltpu.VMEM((tile // LANE, rows, LANE), f32)],
        compiler_params=pltpu.CompilerParams(vmem_limit_bytes=48 << 20),
        cost_estimate=pl.CostEstimate(flops=4 * rows * depth * width, bytes_accessed=4 * depth * width, transcendentals=rows * width),
    )(flat, gate_weight, cand_weight, forget_bias.reshape(1, width), read, scale)
    spans = lax.all_gather(span, "seq", axis=0, tiled=False)
    where = lax.axis_index("seq").astype(jnp.int32).reshape(1)
    dpre, dcand = pl.pallas_call(
        functools.partial(delta_kernel, devices),
        grid=(width // tile,),
        in_specs=[
            pl.BlockSpec(memory_space=pltpu.SMEM),
            pl.BlockSpec((devices, 8, tile), lambda i: (0, 0, i)),
            seg_spec,
            lane,
            lane,
            col,
            full_scale,
        ],
        out_specs=[col, col],
        out_shape=[jax.ShapeDtypeStruct((rows, width), jnp.bfloat16)] * 2,
        scratch_shapes=[pltpu.VMEM((tile // LANE, rows, LANE), f32)] * 3,
        compiler_params=pltpu.CompilerParams(vmem_limit_bytes=48 << 20),
    )(where, spans, seg, keep, cand, read, scale)

    contract0 = (((0,), (0,)), ((), ()))
    contract1 = (((1,), (1,)), ((), ()))
    all_dpre = lax.all_gather(dpre, "seq", axis=0, tiled=True)
    all_dcand = lax.all_gather(dcand, "seq", axis=0, tiled=True)
    term = lax.dot_general(dpre, gate_weight, contract1, preferred_element_type=f32)
    term = term + lax.dot_general(dcand, cand_weight, contract1, preferred_element_type=f32)
    term = term.astype(jnp.bfloat16).reshape(2, count, depth)
    grad_tokens = lax.psum_scatter(term, "tp", scatter_dimension=2, tiled=True)
    grad_gate = lax.dot_general(cols, all_dpre, contract0, preferred_element_type=f32)
    grad_cand = lax.dot_general(cols, all_dcand, contract0, preferred_element_type=f32)
    return (grad_gate, grad_cand, grad_tokens)


def solution(mesh):
    in_specs = (
        P(None, "seq", "tp"),
        P(None, "tp"),
        P(None, "tp"),
        P("tp"),
        P(None, "seq", "tp"),
        P(None, "seq"),
    )
    out_specs = (P("seq", "tp"), P("seq", "tp"), P(None, "seq", "tp"))
    return jax.shard_map(shards, mesh=mesh, in_specs=in_specs, out_specs=out_specs, check_vma=False)
```

time: 680 us -> 311 us (0.46); the launches traced: 671 us -> 311 us
  local copies, waits for them, and re-layouts: 270 us -> 3.61 us
  other arithmetic: 76.9 us -> 0.01 us
  starting transfers between devices: 41.2 us -> 0.38 us
  blocking collectives: 0 us -> 39.7 us
  waiting for transfers between devices: 232 us -> 208 us
  Pallas kernels: 0 us -> 15.5 us
    slice x104 -> x0, local copies, waits for them, and re-layouts: 188 us -> none  [the longest x53 113 us: shards(): lax.associative_scan(compose, (coef, score), reverse=True, axis=1)]
    ppermute x14 -> x0, starting transfers between devices: 35.2 us -> none  [from_behind(): return lax.ppermute(block, axis, route)]
    pad x50 -> x0, local copies, waits for them, and re-layouts: 34.3 us -> none  [the longest x26 20 us: shards(): lax.associative_scan(compose, (coef, score), reverse=True, axis=1)]
    ppermute x14 -> x0, waiting for transfers between devices: 31.7 us -> none  [from_behind(): return lax.ppermute(block, axis, route)]
    mul x28 -> x1, other arithmetic: 31.5 us -> 0.01 us  [shards(): scale = (advantage.astype(jnp.float32) * 0.25).reshape(rows, 1)]
    rev x2 -> x0, local copies, waits for them, and re-layouts: 26.6 us -> none  [shards(): lax.associative_scan(compose, (coef, score), reverse=True, axis=1)]
    all_to_all x0 -> x1, blocking collectives: none -> 25.5 us  [shards(): mine = lax.all_to_all(mine, 'seq', split_axis=1, concat_axis=0, tiled=True)]
    add x41 -> x0, other arithmetic: 25 us -> none  [the longest x13 11.5 us: shards(): lax.associative_scan(compose, (coef, score), reverse=True, axis=1)]
  transfers between devices with their start and end apart: 18 -> 5, of which waited for: 18 -> 4; matrix products, arithmetic and copies ran while one was open for 5% -> 10% of each run, Pallas kernels for 0% -> 5%
where the time goes in v1:
time: 311 us
  waiting for transfers between devices  208 us (67%)
  blocking collectives  39.7 us (13%)
  matrix products  29.9 us (10%)
  Pallas kernels  15.5 us (5%)
  between operations  13.9 us (4%)
  local copies, waits for them, and re-layouts  3.61 us (1%)
    all_gather x1, waiting for transfers between devices, shards(): all_dcand = lax.all_gather(dcand, 'seq', axis=0, tiled=True)  61.2 us
    all_gather x1, waiting for transfers between devices, shards(): all_dpre = lax.all_gather(dpre, 'seq', axis=0, tiled=True)  58 us
    all_gather x1, waiting for transfers between devices, shards(): whole = lax.all_gather(tokens, 'tp', axis=2, tiled=True)  48.6 us
    reduce_scatter x1, waiting for transfers between devices, shards(): grad_tokens = lax.psum_scatter(term, 'tp', scatter_dimension=2, tiled=True)  38.5 us
    all_to_all x1, blocking collectives, shards(): mine = lax.all_to_all(mine, 'seq', split_axis=1, concat_axis=0, tiled=True)  25.5 us
    all_gather x1, blocking collectives, shards(): spans = lax.all_gather(span, 'seq', axis=0, tiled=False)  14.2 us
    pallas_call x1, Pallas kernels, shards(): pl.pallas_call(project_kernel, grid=(width // tile,), in_specs=[pl.BlockS...  12 us
    dot_general x1, matrix products, shards(): lax.dot_general(dcand, cand_weight, contract1, preferred_element_type=f32)  8.75 us
  transfers between devices with their start and end apart: 5, of which 4 were waited for; matrix products, arithmetic and copies ran while one was open for 10% of the time, Pallas kernels for 5%

profile of v1, /device:TPU:0, one launch (start us, length us, event | category | flops | bytes accessed | tf_op | source)
XLA Modules:
  0.0 310.5 jit_solution(3191718958135807867)
XLA Ops:
  7.2 0.0 copy-start.2
  7.2 0.0 copy-start
  7.2 0.0 copy-start.1
  7.2 0.0 all-gather.6.cloned.1.call-start
  7.2 0.7 all-gather.6.cloned.1.call-update
  7.9 0.0 all-gather.8.cloned.1.call-start
  8.0 48.6 %all-gather.6.cloned.1.call-done = bf16[2,192,4096]{2,1,0:T(8,128)(2,1)} async-done(((bf16[2,192,1024]{2,1,0:T(8,128)(2,1)}), bf16[2,192,4096]{2,1,0:T(8,128)(2,1)}) %all-gather.6.cloned.1.call-update) | async-done | bytes 3145744 | tf_op jit(solution)/shard_map/all_gather | solution.py:112
  56.6 1.2 constant_dynamic-slice_fusion
  57.8 0.1 copy.25
  57.8 25.5 %all_to_all.16 = bf16[96,8,512]{2,0,1:T(8,128)(2,1)} all-to-all(bf16[96,8,512]{2,0,1:T(8,128)(2,1)S(1)} %bitcast.35), channel_id=1, replica_groups=mesh['seq'=8,'tp'=4] {'seq'}, dimensions={1} | all-to-all | bytes 1572864 | tf_op jit(solution)/shard_map/all_to_all | solution.py:120
  83.3 0.0 all-gather.8.cloned.1.call-update
  83.4 0.0 all-gather.12.cloned.1.call-start
  83.4 0.0 copy-done.2
  83.4 0.2 reshape.43.scale
  83.6 0.0 copy-done
  83.7 0.0 copy-done.1
  83.7 12.0 %shard_map.85 = (f32[8,384,128]{2,1,0:T(8,128)S(1)}, f32[8,384,128]{2,1,0:T(8,128)S(1)}, f32[3,2,8,1024]{3,2,1,0:T(8,128)S(1)}, f32[8,1024]{1,0:T(8,128)S(1)}) custom-call(bf16[384,4096]{1,0:T(8,128)(2,1)} %bitcast.37, bf16[4096,1024]{1,0:T(8,128)(2,1)} %gate.1, bf16[4096,1024]{1,0:T(8,128)(2,1)} %cand_w.1, f32[1,1024]{1,0:T(1,128)S(1)} %bitcast.28, ...), custom_call_target="tpu_custom_call" | custom-call | flops 6442450944 | bytes 16777216 | tf_op jit(solution)/shard_map/pallas_call | solution.py:133
  95.7 14.2 %all-gather = f32[64,1024]{1,0:T(8,128)S(1)} all-gather(f32[8,1024]{1,0:T(8,128)S(1)} %get-tuple-element.9), channel_id=2, replica_groups=mesh['seq'=8,'tp'=4] {'seq'}, dimensions={0}, use_global_device_ids=true | all-gather | bytes 294912 | tf_op jit(solution)/shard_map/all_gather | solution.py:155
  109.9 3.5 %shard_map.86 = (bf16[384,1024]{1,0:T(8,128)(2,1)}, bf16[384,1024]{1,0:T(8,128)(2,1)}) custom-call(s32[1]{0:T(128)} %bitcast.6.where, f32[8,8,1024]{2,1,0:T(8,128)S(1)} %bitcast.25, f32[3,2,8,1024]{3,2,1,0:T(8,128)S(1)} %get-tuple-element.10.seg, f32[8,384,128]{2,1,0:T(8,128)S(1)} %get-tuple-element.11.keep, f32[8,384,128]{2,1,0:T(8,128)S(1)} %get-tuple-element.12.cand, ...), custom_call_target="tpu_custom_call" | custom-call | tf_op jit(solution)/shard_map/pallas_call | solution.py:157
  113.4 0.0 all-gather.12.cloned.1.call-update
  113.4 0.0 all-gather.10.cloned.1.call-start
  113.5 0.5 all-gather.10.cloned.1.call-update
  114.0 0.2 reduce-scatter.2.cloned.1.call-start
  114.2 6.1 %fusion.2 = f32[384,4096]{1,0:T(8,128)S(1)} fusion(bf16[384,1024]{1,0:T(8,128)(2,1)} %get-tuple-element.13, bf16[4096,1024]{1,0:T(8,128)(2,1)} %gate.1), kind=kOutput, calls=%fused_computation.6 | convolution fusion | flops 3221225472 | bytes 15466496 | tf_op jit(solution)/shard_map/dot_general | solution.py:179
  120.3 8.8 %add_convert_fusion = bf16[384,4096]{1,0:T(8,128)(2,1)} fusion(f32[384,4096]{1,0:T(8,128)S(1)} %fusion.2, bf16[384,1024]{1,0:T(8,128)(2,1)} %get-tuple-element.14, bf16[4096,1024]{1,0:T(8,128)(2,1)} %cand_w.1), kind=kOutput, calls=%fused_computation | convolution fusion | flops 3224371200 | bytes 18612224 | tf_op jit(solution)/shard_map/dot_general | solution.py:180
  129.1 0.0 reduce-scatter.2.cloned.1.call-update
  129.1 0.0 all-gather.8.cloned.1.call-done
  129.1 2.1 copy.20
  131.3 61.2 %all-gather.12.cloned.1.call-done = bf16[3072,1024]{1,0:T(8,128)(2,1)} async-done(((bf16[384,1024]{1,0:T(8,128)(2,1)}), bf16[3072,1024]{1,0:T(8,128)(2,1)}) %all-gather.12.cloned.1.call-update) | async-done | bytes 6291472 | tf_op jit(solution)/shard_map/all_gather | solution.py:178
  192.4 7.5 %fusion.1 = f32[512,1024]{1,0:T(8,128)} fusion(bf16[3072,512]{1,0:T(8,128)(2,1)S(1)} %bitcast.31, bf16[3072,1024]{1,0:T(8,128)(2,1)} %all-gather.12.cloned.1.call-done), kind=kOutput, calls=%fused_computation.5 | convolution fusion | flops 3221225472 | bytes 11534336 | tf_op jit(solution)/shard_map/dot_general | solution.py:184
  200.0 58.0 %all-gather.10.cloned.1.call-done = bf16[3072,1024]{1,0:T(8,128)(2,1)} async-done(((bf16[384,1024]{1,0:T(8,128)(2,1)}), bf16[3072,1024]{1,0:T(8,128)(2,1)}) %all-gather.10.cloned.1.call-update) | async-done | bytes 6291472 | tf_op jit(solution)/shard_map/all_gather | solution.py:177
  257.9 7.5 %fusion = f32[512,1024]{1,0:T(8,128)} fusion(bf16[3072,512]{1,0:T(8,128)(2,1)S(1)} %bitcast.32, bf16[3072,1024]{1,0:T(8,128)(2,1)} %all-gather.10.cloned.1.call-done), kind=kOutput, calls=%fused_computation.4 | convolution fusion | flops 3221225472 | bytes 11534336 | tf_op jit(solution)/shard_map/dot_general | solution.py:183
  265.5 38.5 %reduce-scatter.2.cloned.1.call-done = bf16[2,192,1024]{2,1,0:T(8,128)(2,1)} async-done(((bf16[2,192,4096]{2,1,0:T(8,128)(2,1)}), bf16[2,192,1024]{2,1,0:T(8,128)(2,1)}) %reduce-scatter.2.cloned.1.call-update) | async-done | bytes 786448 | tf_op jit(solution)/shard_map/reduce_scatter | solution.py:182
  (1 shorter events, 0.0 us)
Async XLA Ops:
  7.2 76.2 %copy-start.2 = (s32[2,192]{1,0:T(2,128)S(1)}, s32[2,192]{1,0:T(2,128)}, u32[]{:S(2)}) copy-start(s32[2,192]{1,0:T(2,128)} %param.11) | copy-start | bytes 4612
  7.2 76.5 %copy-start = (bf16[2,192,1024]{2,1,0:T(8,128)(2,1)S(1)}, bf16[2,192,1024]{2,1,0:T(8,128)(2,1)}, u32[]{:S(2)}) copy-start(bf16[2,192,1024]{2,1,0:T(8,128)(2,1)} %param.10) | copy-start | bytes 2359300
  7.2 76.5 %copy-start.1 = (f32[1024]{0:T(1024)S(1)}, f32[1024]{0:T(1024)}, u32[]{:S(2)}) copy-start(f32[1024]{0:T(1024)} %param.9) | copy-start | bytes 12292
  7.2 49.4 %all-gather.6.cloned.1.call-start = ((), (), s32[]{:S(2)}) async-start(), calls=%async_computation.2 | async-start | bytes 3932160 | tf_op jit(solution)/shard_map/all_gather | solution.py:112
  7.9 121.2 %all-gather.8.cloned.1.call-start = ((), (), s32[]{:S(2)}) async-start(), calls=%async_computation.3 | async-start | bytes 3932160 | tf_op jit(solution)/shard_map/all_gather | solution.py:121
  83.4 109.1 %all-gather.12.cloned.1.call-start = ((), (), s32[]{:S(2)}) async-start(), calls=%async_computation.5 | async-start | bytes 7077888 | tf_op jit(solution)/shard_map/all_gather | solution.py:178
  113.4 144.5 %all-gather.10.cloned.1.call-start = ((), (), s32[]{:S(2)}) async-start(), calls=%async_computation.4 | async-start | bytes 7077888 | tf_op jit(solution)/shard_map/all_gather | solution.py:177
  114.0 190.0 %reduce-scatter.2.cloned.1.call-start = ((), (), s32[]{:S(2)}) async-start(), calls=%async_computation.6 | async-start | bytes 3932160 | tf_op jit(solution)/shard_map/reduce_scatter | solution.py:182
Sparse Core Ops, SparseCore 0:
  9.9 46.6 all-gather.5
  83.5 41.8 all-gather.7
  127.6 64.7 all-gather.11
  194.5 63.3 all-gather.9
  261.3 42.5 reduce-scatter.1

commit v2 on v1

--- a/solution.py
+++ b/solution.py
@@ -57,7 +57,7 @@
         span_out[4 + b : 5 + b, at] = r
 
 
-def delta_kernel(devices, where, spans, seg, keep, cand, read, scale, dpre_out, dcand_out, score, dp, dc):
+def delta_kernel(devices, where, spans, seg, keep, cand, read, scale, delta_out, score, dp, dc):
     lanes, rows_all, _ = keep.shape
     count = rows_all // 2
     steps = count // SEGS
@@ -102,8 +102,118 @@
             tails[p] = k * adj
     for l in range(lanes):
         at = slice(l * LANE, (l + 1) * LANE)
-        dpre_out[:, at] = dp[l].astype(jnp.bfloat16)
-        dcand_out[:, at] = dc[l].astype(jnp.bfloat16)
+        delta_out[0, :, at] = dp[l].astype(jnp.bfloat16)
+        delta_out[1, :, at] = dc[l].astype(jnp.bfloat16)
+
+
+def exchange_kernel(chips, groups, delta, cols, gate_hbm, cand_hbm, gate_out, cand_out, tok_out,
+                    slots, weights, partial, landed, w_sem, own_sem, send_sem, pass_sem, recv_sem, part_send, part_recv):
+    seq = lax.axis_index("seq")
+    tp = lax.axis_index("tp")
+    chip = lax.div(seq, 2)
+    core = lax.rem(seq, 2)
+    sibling = chip * 2 + 1 - core
+    block = weights.shape[2]
+    mesh_id = pl.DeviceIdType.MESH
+
+    barrier = pltpu.get_barrier_semaphore()
+    for d in range(1, chips):
+        other = lax.rem(chip + d, chips) * 2 + core
+        pl.semaphore_signal(barrier, inc=1, device_id=(other, tp), device_id_type=mesh_id)
+    pl.semaphore_signal(barrier, inc=1, device_id=(sibling, tp), device_id_type=mesh_id)
+    for d in range(1, groups):
+        pl.semaphore_signal(barrier, inc=1, device_id=(seq, lax.rem(tp + d, groups)), device_id_type=mesh_id)
+
+    def fetch(p, buf):
+        rows = pl.ds(pl.multiple_of(lax.rem(tp + p, groups) * block, 128), block)
+        return [
+            pltpu.make_async_copy(w.at[rows, :], weights.at[buf, k], w_sem.at[buf, k])
+            for k, w in enumerate((gate_hbm, cand_hbm))
+        ]
+
+    for copy in fetch(1 % groups, 0):
+        copy.start()
+    pl.semaphore_wait(barrier, chips - 1 + 1 + groups - 1)
+
+    def send(kind, d):
+        other = lax.rem(chip + d, chips) * 2 + core
+        return pltpu.make_async_remote_copy(
+            src_ref=delta.at[kind], dst_ref=slots.at[seq, kind], send_sem=send_sem.at[kind, d],
+            recv_sem=recv_sem.at[seq, kind], device_id=(other, tp), device_id_type=mesh_id)
+
+    def receive(kind, origin):
+        return pltpu.make_async_remote_copy(
+            src_ref=delta.at[kind], dst_ref=slots.at[origin, kind], send_sem=send_sem.at[kind, 0],
+            recv_sem=recv_sem.at[origin, kind], device_id=(sibling, tp), device_id_type=mesh_id)
+
+    def hand(kind, d):
+        origin = lax.rem(chip + d, chips) * 2 + core
+        return pltpu.make_async_remote_copy(
+            src_ref=slots.at[origin, kind], dst_ref=slots.at[origin, kind], send_sem=pass_sem.at[kind, d],
+            recv_sem=recv_sem.at[origin, kind], device_id=(sibling, tp), device_id_type=mesh_id)
+
+    def own(kind):
+        return pltpu.make_async_copy(delta.at[kind], slots.at[seq, kind], own_sem.at[kind])
+
+    for kind in range(2):
+        own(kind).start()
+        for d in range(1, chips):
+            send(kind, d).start()
+    for kind in range(2):
+        own(kind).wait()
+        hand(kind, 0).start()
+
+    nt = (((1,), (1,)), ((), ()))
+    tn = (((0,), (0,)), ((), ()))
+    f32 = jnp.float32
+
+    def share(p, buf):
+        for copy in fetch(p, buf):
+            copy.wait()
+        term = lax.dot_general(delta[0], weights[buf, 0], nt, preferred_element_type=f32)
+        return term + lax.dot_general(delta[1], weights[buf, 1], nt, preferred_element_type=f32)
+
+    def give(p):
+        return pltpu.make_async_remote_copy(
+            src_ref=partial.at[p - 1], dst_ref=landed.at[p - 1], send_sem=part_send.at[p - 1],
+            recv_sem=part_recv.at[p - 1], device_id=(seq, lax.rem(tp + p, groups)), device_id_type=mesh_id)
+
+    for p in range(1, groups):
+        for copy in fetch((p + 1) % groups, p % 2):
+            copy.start()
+        partial[p - 1] = share(p, (p - 1) % 2).astype(jnp.bfloat16)
+        give(p).start()
+    mine = share(0, (groups - 1) % 2)
+    for p in range(1, groups):
+        give(p).wait()
+        mine = mine + landed[p - 1].astype(f32)
+    tok_out[...] = mine.astype(jnp.bfloat16)
+
+    gate_out[...] = jnp.zeros_like(gate_out)
+    cand_out[...] = jnp.zeros_like(cand_out)
+    for kind, out in enumerate((gate_out, cand_out)):
+
+        def step(d, carry):
+            at = lax.rem(chip + d, chips) * 2
+            lane = at + core
+
+            @pl.when(d > 0)
+            def _():
+                receive(kind, lane).wait_recv()
+                hand(kind, d).start()
+
+            out[...] += lax.dot_general(cols[lane], slots[lane, kind], tn, preferred_element_type=f32)
+            other = at + 1 - core
+            receive(kind, other).wait_recv()
+            out[...] += lax.dot_general(cols[other], slots[other, kind], tn, preferred_element_type=f32)
+            return carry
+
+        lax.fori_loop(0, chips, step, 0)
+    for kind in range(2):
+        for d in range(chips):
+            if d > 0:
+                send(kind, d).wait_send()
+            hand(kind, d).wait_send()
 
 
 def shards(tokens, gate_weight, cand_weight, forget_bias, readout, advantage):
@@ -120,7 +230,7 @@
     mine = lax.all_to_all(mine, "seq", split_axis=1, concat_axis=0, tiled=True)
     cols = lax.all_gather(mine, "tp", axis=0, tiled=False)
     cols = cols.reshape(groups, devices, part, depth // devices)
-    cols = jnp.transpose(cols, (1, 0, 2, 3)).reshape(devices * rows, depth // devices)
+    cols = jnp.transpose(cols, (1, 0, 2, 3)).reshape(devices, rows, depth // devices)
 
     scale = (advantage.astype(jnp.float32) * 0.25).reshape(rows, 1)
     read = readout.reshape(rows, width)
@@ -154,7 +264,7 @@
     )(flat, gate_weight, cand_weight, forget_bias.reshape(1, width), read, scale)
     spans = lax.all_gather(span, "seq", axis=0, tiled=False)
     where = lax.axis_index("seq").astype(jnp.int32).reshape(1)
-    dpre, dcand = pl.pallas_call(
+    delta = pl.pallas_call(
         functools.partial(delta_kernel, devices),
         grid=(width // tile,),
         in_specs=[
@@ -166,23 +276,43 @@
             col,
             full_scale,
         ],
-        out_specs=[col, col],
-        out_shape=[jax.ShapeDtypeStruct((rows, width), jnp.bfloat16)] * 2,
+        out_specs=pl.BlockSpec((2, rows, tile), lambda i: (0, 0, i)),
+        out_shape=jax.ShapeDtypeStruct((2, rows, width), jnp.bfloat16),
         scratch_shapes=[pltpu.VMEM((tile // LANE, rows, LANE), f32)] * 3,
         compiler_params=pltpu.CompilerParams(vmem_limit_bytes=48 << 20),
     )(where, spans, seg, keep, cand, read, scale)
 
-    contract0 = (((0,), (0,)), ((), ()))
-    contract1 = (((1,), (1,)), ((), ()))
-    all_dpre = lax.all_gather(dpre, "seq", axis=0, tiled=True)
-    all_dcand = lax.all_gather(dcand, "seq", axis=0, tiled=True)
-    term = lax.dot_general(dpre, gate_weight, contract1, preferred_element_type=f32)
-    term = term + lax.dot_general(dcand, cand_weight, contract1, preferred_element_type=f32)
-    term = term.astype(jnp.bfloat16).reshape(2, count, depth)
-    grad_tokens = lax.psum_scatter(term, "tp", scatter_dimension=2, tiled=True)
-    grad_gate = lax.dot_general(cols, all_dpre, contract0, preferred_element_type=f32)
-    grad_cand = lax.dot_general(cols, all_dcand, contract0, preferred_element_type=f32)
-    return (grad_gate, grad_cand, grad_tokens)
+    chips = devices // 2
+    block = depth // groups
+    bf16 = jnp.bfloat16
+    dma = pltpu.SemaphoreType.DMA
+    vmem = pl.BlockSpec(memory_space=pltpu.VMEM)
+    grad_gate, grad_cand, grad_tokens = pl.pallas_call(
+        functools.partial(exchange_kernel, chips, groups),
+        in_specs=[vmem, vmem, pl.BlockSpec(memory_space=pl.ANY), pl.BlockSpec(memory_space=pl.ANY)],
+        out_specs=[vmem, vmem, vmem],
+        out_shape=[
+            jax.ShapeDtypeStruct((depth // devices, width), f32),
+            jax.ShapeDtypeStruct((depth // devices, width), f32),
+            jax.ShapeDtypeStruct((rows, block), bf16),
+        ],
+        scratch_shapes=[
+            pltpu.VMEM((devices, 2, rows, width), bf16),
+            pltpu.VMEM((2, 2, block, width), bf16),
+            pltpu.VMEM((groups - 1, rows, block), bf16),
+            pltpu.VMEM((groups - 1, rows, block), bf16),
+            dma((2, 2)),
+            dma((2,)),
+            dma((2, chips)),
+            dma((2, chips)),
+            dma((devices, 2)),
+            dma((groups - 1,)),
+            dma((groups - 1,)),
+        ],
+        compiler_params=pltpu.CompilerParams(collective_id=1, has_side_effects=True, vmem_limit_bytes=56 << 20),
+        cost_estimate=pl.CostEstimate(flops=12 * rows * depth * width, bytes_accessed=24 << 20, transcendentals=0),
+    )(delta, cols, gate_weight, cand_weight)
+    return (grad_gate, grad_cand, grad_tokens.reshape(2, count, block))
 
 
 def solution(mesh):

time: 311 us -> 293 us (0.942)
  the two profiles are of different devices: /device:TPU:0 before, /device:TPU:9 now
where the time goes in v2:
time: 293 us
  Pallas kernels  167 us (57%)
  waiting for transfers between devices  60.7 us (21%)
  blocking collectives  38.4 us (13%)
  between operations  14.2 us (5%)
  local copies, waits for them, and re-layouts  12.3 us (4%)
    pallas_call x1, Pallas kernels, shards(): pl.pallas_call(functools.partial(exchange_kernel, chips, groups), in_spec...  152 us
    all_gather x1, waiting for transfers between devices, shards(): whole = lax.all_gather(tokens, 'tp', axis=2, tiled=True)  47.1 us
    all_to_all x1, blocking collectives, shards(): mine = lax.all_to_all(mine, 'seq', split_axis=1, concat_axis=0, tiled=True)  23.3 us
    all_gather x1, blocking collectives, shards(): spans = lax.all_gather(span, 'seq', axis=0, tiled=False)  15 us
    all_gather x1, waiting for transfers between devices, shards(): cols = lax.all_gather(mine, 'tp', axis=0, tiled=False)  12.9 us
    pallas_call x1, Pallas kernels, shards(): pl.pallas_call(project_kernel, grid=(width // tile,), in_specs=[pl.BlockS...  12.1 us
    unnamed x15, local copies, waits for them, and re-layouts  7.02 us
  transfers between devices with their start and end apart: 2, of which 2 were waited for; matrix products, arithmetic and copies ran while one was open for 0% of the time, Pallas kernels for 5%

profile of v2, /device:TPU:9, one launch (start us, length us, event | category | flops | bytes accessed | tf_op | source)
XLA Modules:
  0.0 292.6 jit_solution(16761878185457202176)
XLA Ops:
  7.2 0.0 all-gather.4.cloned.1.call-start
  7.2 0.7 all-gather.4.cloned.1.call-update
  7.9 0.0 all-gather.6.cloned.1.call-start
  7.9 47.1 %all-gather.4.cloned.1.call-done = bf16[2,192,4096]{2,1,0:T(8,128)(2,1)} async-done(((bf16[2,192,1024]{2,1,0:T(8,128)(2,1)}), bf16[2,192,4096]{2,1,0:T(8,128)(2,1)}) %all-gather.4.cloned.1.call-update) | async-done | bytes 3145744 | tf_op jit(solution)/shard_map/all_gather | solution.py:222
  55.0 1.2 constant_dynamic-slice_fusion
  56.2 0.0 copy-start.5
  56.2 0.0 copy-start.1
  56.2 0.0 copy-start.2
  56.2 0.1 copy.22
  56.3 23.3 %all_to_all.16 = bf16[96,8,512]{2,0,1:T(8,128)(2,1)} all-to-all(bf16[96,8,512]{2,0,1:T(8,128)(2,1)S(1)} %bitcast.25), channel_id=1, replica_groups=mesh['seq'=8,'tp'=4] {'seq'}, dimensions={1} | all-to-all | bytes 1572864 | tf_op jit(solution)/shard_map/all_to_all | solution.py:230
  79.7 0.0 all-gather.6.cloned.1.call-update
  79.7 0.0 copy-done.5
  79.7 0.2 reshape.43.scale
  79.9 0.0 copy-done.1
  79.9 0.0 copy-done.2
  79.9 12.1 %shard_map.85 = (f32[8,384,128]{2,1,0:T(8,128)S(1)}, f32[8,384,128]{2,1,0:T(8,128)S(1)}, f32[3,2,8,1024]{3,2,1,0:T(8,128)S(1)}, f32[8,1024]{1,0:T(8,128)S(1)}) custom-call(bf16[384,4096]{1,0:T(8,128)(2,1)} %bitcast.28, bf16[4096,1024]{1,0:T(8,128)(2,1)} %gate_hbm.1, bf16[4096,1024]{1,0:T(8,128)(2,1)} %cand_hbm.1, f32[1,1024]{1,0:T(1,128)S(1)} %bitcast.20, ...), custom_call_target="tpu_custom_call" | custom-call | flops 6442450944 | bytes 16777216 | tf_op jit(solution)/shard_map/pallas_call | solution.py:243
  92.1 15.0 %all-gather = f32[64,1024]{1,0:T(8,128)S(1)} all-gather(f32[8,1024]{1,0:T(8,128)S(1)} %get-tuple-element.10), channel_id=2, replica_groups=mesh['seq'=8,'tp'=4] {'seq'}, dimensions={0}, use_global_device_ids=true | all-gather | bytes 294912 | tf_op jit(solution)/shard_map/all_gather | solution.py:265
  107.1 2.8 shard_map.86.delta
  110.0 0.0 copy-start
  110.0 1.1 copy-done
  111.1 12.9 %all-gather.6.cloned.1.call-done = bf16[4,768,512]{2,1,0:T(8,128)(2,1)} async-done(((bf16[1,768,512]{2,1,0:T(8,128)(2,1)}), bf16[4,768,512]{2,1,0:T(8,128)(2,1)}) %all-gather.6.cloned.1.call-update) | async-done | bytes 3145744 | tf_op jit(solution)/shard_map/all_gather | solution.py:231
  124.0 3.9 %copy.19 = bf16[8,4,96,512]{3,2,1,0:T(8,128)(2,1)} copy(bf16[8,4,96,512]{3,2,0,1:T(8,128)(2,1)} %bitcast.21) | data formatting | bytes 6291456 | tf_op jit(solution)/shard_map/transpose | solution.py:233
  127.9 152.0 %shard_map.87 = (f32[512,1024]{1,0:T(8,128)}, f32[512,1024]{1,0:T(8,128)}, bf16[384,1024]{1,0:T(8,128)(2,1)}) custom-call(bf16[2,384,1024]{2,1,0:T(8,128)(2,1)} %copy-done, bf16[8,384,512]{2,1,0:T(8,128)(2,1)} %bitcast.22, bf16[4096,1024]{1,0:T(8,128)(2,1)} %gate_hbm.1, bf16[4096,1024]{1,0:T(8,128)(2,1)} %cand_hbm.1), custom_call_target="tpu_custom_call" | custom-call | flops 19327352832 | bytes 25165824 | tf_op jit(solution)/shard_map/pallas_call | solution.py:290
  279.9 0.0 copy-start.3
  279.9 3.3 %copy.26 = f32[512,1024]{1,0:T(8,128)} copy(f32[512,1024]{1,0:T(8,128)} %get-tuple-element.20) | data formatting | bytes 4194304
  283.2 0.0 copy-done.3
  283.2 0.0 copy-start.4
  283.2 1.3 copy.27
  284.6 0.4 copy-done.4
  284.9 0.9 copy.28
  (1 shorter events, 0.0 us)
Async XLA Ops:
  7.2 47.9 %all-gather.4.cloned.1.call-start = ((), (), s32[]{:S(2)}) async-start(), calls=%async_computation.1 | async-start | bytes 3932160 | tf_op jit(solution)/shard_map/all_gather | solution.py:222
  7.9 116.1 %all-gather.6.cloned.1.call-start = ((), (), s32[]{:S(2)}) async-start(), calls=%async_computation.2 | async-start | bytes 3932160 | tf_op jit(solution)/shard_map/all_gather | solution.py:231
  56.2 23.5 %copy-start.5 = (s32[2,192]{1,0:T(2,128)S(1)}, s32[2,192]{1,0:T(2,128)}, u32[]{:S(2)}) copy-start(s32[2,192]{1,0:T(2,128)} %param.11) | copy-start | bytes 4612
  56.2 23.7 %copy-start.1 = (bf16[2,192,1024]{2,1,0:T(8,128)(2,1)S(1)}, bf16[2,192,1024]{2,1,0:T(8,128)(2,1)}, u32[]{:S(2)}) copy-start(bf16[2,192,1024]{2,1,0:T(8,128)(2,1)} %param.10) | copy-start | bytes 2359300
  56.2 23.7 %copy-start.2 = (f32[1024]{0:T(1024)S(1)}, f32[1024]{0:T(1024)}, u32[]{:S(2)}) copy-start(f32[1024]{0:T(1024)} %param.9) | copy-start | bytes 12292
  110.0 1.1 copy-start
  279.9 3.3 %copy-start.3 = (f32[512,1024]{1,0:T(8,128)S(1)}, f32[512,1024]{1,0:T(8,128)}, u32[]{:S(2)}) copy-start(f32[512,1024]{1,0:T(8,128)} %get-tuple-element.21) | copy-start | bytes 6291460
  283.2 1.7 copy-start.4
Sparse Core Ops, SparseCore 0:
  9.8 45.1 all-gather.3
  79.8 44.1 all-gather.5

commit v3 on v2

--- a/solution.py
+++ b/solution.py
@@ -107,7 +107,7 @@
 
 
 def exchange_kernel(chips, groups, delta, cols, gate_hbm, cand_hbm, gate_out, cand_out, tok_out,
-                    slots, weights, partial, landed, w_sem, own_sem, send_sem, pass_sem, recv_sem, part_send, part_recv):
+                    slots, weights, partial, landed, w_sem, own_sem, pass_sem, recv_sem, part_send, part_recv):
     seq = lax.axis_index("seq")
     tp = lax.axis_index("tp")
     chip = lax.div(seq, 2)
@@ -116,10 +116,19 @@
     block = weights.shape[2]
     mesh_id = pl.DeviceIdType.MESH
 
+    last = chips - 1
+    right = jnp.minimum(chip + 1, last) * 2 + core
+    left = jnp.maximum(chip - 1, 0) * 2 + core
     barrier = pltpu.get_barrier_semaphore()
-    for d in range(1, chips):
-        other = lax.rem(chip + d, chips) * 2 + core
-        pl.semaphore_signal(barrier, inc=1, device_id=(other, tp), device_id_type=mesh_id)
+
+    @pl.when(chip < last)
+    def _():
+        pl.semaphore_signal(barrier, inc=1, device_id=(right, tp), device_id_type=mesh_id)
+
+    @pl.when(chip > 0)
+    def _():
+        pl.semaphore_signal(barrier, inc=1, device_id=(left, tp), device_id_type=mesh_id)
+
     pl.semaphore_signal(barrier, inc=1, device_id=(sibling, tp), device_id_type=mesh_id)
     for d in range(1, groups):
         pl.semaphore_signal(barrier, inc=1, device_id=(seq, lax.rem(tp + d, groups)), device_id_type=mesh_id)
@@ -133,35 +142,30 @@
 
     for copy in fetch(1 % groups, 0):
         copy.start()
-    pl.semaphore_wait(barrier, chips - 1 + 1 + groups - 1)
-
-    def send(kind, d):
-        other = lax.rem(chip + d, chips) * 2 + core
+    pl.semaphore_wait(barrier, groups + jnp.minimum(chip, 1) + jnp.minimum(last - chip, 1))
+
+    def pass_on(kind, origin, target, way):
         return pltpu.make_async_remote_copy(
-            src_ref=delta.at[kind], dst_ref=slots.at[seq, kind], send_sem=send_sem.at[kind, d],
-            recv_sem=recv_sem.at[seq, kind], device_id=(other, tp), device_id_type=mesh_id)
-
-    def receive(kind, origin):
-        return pltpu.make_async_remote_copy(
-            src_ref=delta.at[kind], dst_ref=slots.at[origin, kind], send_sem=send_sem.at[kind, 0],
-            recv_sem=recv_sem.at[origin, kind], device_id=(sibling, tp), device_id_type=mesh_id)
-
-    def hand(kind, d):
-        origin = lax.rem(chip + d, chips) * 2 + core
-        return pltpu.make_async_remote_copy(
-            src_ref=slots.at[origin, kind], dst_ref=slots.at[origin, kind], send_sem=pass_sem.at[kind, d],
-            recv_sem=recv_sem.at[origin, kind], device_id=(sibling, tp), device_id_type=mesh_id)
+            src_ref=slots.at[origin, kind], dst_ref=slots.at[origin, kind], send_sem=pass_sem.at[way, origin, kind],
+            recv_sem=recv_sem.at[origin, kind], device_id=(target, tp), device_id_type=mesh_id)
 
     def own(kind):
         return pltpu.make_async_copy(delta.at[kind], slots.at[seq, kind], own_sem.at[kind])
 
     for kind in range(2):
         own(kind).start()
-        for d in range(1, chips):
-            send(kind, d).start()
     for kind in range(2):
         own(kind).wait()
-        hand(kind, 0).start()
+
+        @pl.when(chip < last)
+        def _():
+            pass_on(kind, seq, right, 0).start()
+
+        @pl.when(chip > 0)
+        def _():
+            pass_on(kind, seq, left, 1).start()
+
+        pass_on(kind, seq, sibling, 2).start()
 
     nt = (((1,), (1,)), ((), ()))
     tn = (((0,), (0,)), ((), ()))
@@ -193,27 +197,57 @@
     cand_out[...] = jnp.zeros_like(cand_out)
     for kind, out in enumerate((gate_out, cand_out)):
 
-        def step(d, carry):
-            at = lax.rem(chip + d, chips) * 2
-            lane = at + core
-
-            @pl.when(d > 0)
+        def take(origin):
+            out[...] += lax.dot_general(cols[origin], slots[origin, kind], tn, preferred_element_type=f32)
+
+        take(seq)
+        pass_on(kind, sibling, sibling, 2).wait_recv()
+        take(sibling)
+
+        def step(e, carry):
+            dist = lax.div(e, 2) + 1
+            from_left = lax.rem(e, 2) == 0
+            origin_chip = jnp.where(from_left, chip - dist, chip + dist)
+
+            @pl.when((origin_chip >= 0) & (origin_chip <= last))
             def _():
-                receive(kind, lane).wait_recv()
-                hand(kind, d).start()
-
-            out[...] += lax.dot_general(cols[lane], slots[lane, kind], tn, preferred_element_type=f32)
-            other = at + 1 - core
-            receive(kind, other).wait_recv()
-            out[...] += lax.dot_general(cols[other], slots[other, kind], tn, preferred_element_type=f32)
+                origin = origin_chip * 2 + core
+                pass_on(kind, origin, sibling, 2).wait_recv()
+
+                @pl.when(from_left & (chip < last))
+                def _():
+                    pass_on(kind, origin, right, 0).start()
+
+                @pl.when(jnp.logical_not(from_left) & (chip > 0))
+                def _():
+                    pass_on(kind, origin, left, 1).start()
+
+                pass_on(kind, origin, sibling, 2).start()
+                take(origin)
+                other = origin_chip * 2 + 1 - core
+                pass_on(kind, other, sibling, 2).wait_recv()
+                take(other)
+
             return carry
 
-        lax.fori_loop(0, chips, step, 0)
+        lax.fori_loop(0, 2 * last, step, 0)
     for kind in range(2):
-        for d in range(chips):
-            if d > 0:
-                send(kind, d).wait_send()
-            hand(kind, d).wait_send()
+
+        def drain(o, carry):
+            origin = o * 2 + core
+
+            @pl.when((o <= chip) & (chip < last))
+            def _():
+                pass_on(kind, origin, right, 0).wait_send()
+
+            @pl.when((o >= chip) & (chip > 0))
+            def _():
+                pass_on(kind, origin, left, 1).wait_send()
+
+            pass_on(kind, origin, sibling, 2).wait_send()
+            return carry
+
+        lax.fori_loop(0, chips, drain, 0)
 
 
 def shards(tokens, gate_weight, cand_weight, forget_bias, readout, advantage):
@@ -303,8 +337,7 @@
             pltpu.VMEM((groups - 1, rows, block), bf16),
             dma((2, 2)),
             dma((2,)),
-            dma((2, chips)),
-            dma((2, chips)),
+            dma((3, devices, 2)),
             dma((devices, 2)),
             dma((groups - 1,)),
             dma((groups - 1,)),

time: 293 us -> 267 us (0.911)
  the two profiles are of different devices: /device:TPU:9 before, /device:TPU:0 now
where the time goes in v3:
time: 267 us; the launch traced here: 266 us
  Pallas kernels  139 us (52%)
  waiting for transfers between devices  60.9 us (23%)
  blocking collectives  39.8 us (15%)
  between operations  14.2 us (5%)
  local copies, waits for them, and re-layouts  12.3 us (5%)
    pallas_call x1, Pallas kernels, shards(): pl.pallas_call(functools.partial(exchange_kernel, chips, groups), in_spec...  124 us
    all_gather x1, waiting for transfers between devices, shards(): whole = lax.all_gather(tokens, 'tp', axis=2, tiled=True)  48.6 us
    all_to_all x1, blocking collectives, shards(): mine = lax.all_to_all(mine, 'seq', split_axis=1, concat_axis=0, tiled=True)  25.6 us
    all_gather x1, blocking collectives, shards(): spans = lax.all_gather(span, 'seq', axis=0, tiled=False)  14.2 us
    pallas_call x1, Pallas kernels, shards(): pl.pallas_call(project_kernel, grid=(width // tile,), in_specs=[pl.BlockS...  12 us
    all_gather x1, waiting for transfers between devices, shards(): cols = lax.all_gather(mine, 'tp', axis=0, tiled=False)  11.6 us
    unnamed x15, local copies, waits for them, and re-layouts  7.02 us
  transfers between devices with their start and end apart: 2, of which 2 were waited for; matrix products, arithmetic and copies ran while one was open for 0% of the time, Pallas kernels for 6%

profile of v3, /device:TPU:0, one launch (start us, length us, event | category | flops | bytes accessed | tf_op | source)
XLA Modules:
  0.0 266.4 jit_solution(18313022811476949279)
XLA Ops:
  7.2 0.0 all-gather.4.cloned.1.call-start
  7.2 0.7 all-gather.4.cloned.1.call-update
  7.9 0.0 all-gather.6.cloned.1.call-start
  7.9 48.6 %all-gather.4.cloned.1.call-done = bf16[2,192,4096]{2,1,0:T(8,128)(2,1)} async-done(((bf16[2,192,1024]{2,1,0:T(8,128)(2,1)}), bf16[2,192,4096]{2,1,0:T(8,128)(2,1)}) %all-gather.4.cloned.1.call-update) | async-done | bytes 3145744 | tf_op jit(solution)/shard_map/all_gather | solution.py:256
  56.6 1.2 constant_dynamic-slice_fusion
  57.7 0.0 copy-start.5
  57.8 0.0 copy-start.1
  57.8 0.0 copy-start.2
  57.8 0.1 copy.22
  57.9 25.6 %all_to_all.16 = bf16[96,8,512]{2,0,1:T(8,128)(2,1)} all-to-all(bf16[96,8,512]{2,0,1:T(8,128)(2,1)S(1)} %bitcast.25), channel_id=1, replica_groups=mesh['seq'=8,'tp'=4] {'seq'}, dimensions={1} | all-to-all | bytes 1572864 | tf_op jit(solution)/shard_map/all_to_all | solution.py:264
  83.5 0.0 all-gather.6.cloned.1.call-update
  83.5 0.0 copy-done.5
  83.5 0.2 reshape.43.scale
  83.7 0.0 copy-done.1
  83.7 0.0 copy-done.2
  83.7 12.0 %shard_map.85 = (f32[8,384,128]{2,1,0:T(8,128)S(1)}, f32[8,384,128]{2,1,0:T(8,128)S(1)}, f32[3,2,8,1024]{3,2,1,0:T(8,128)S(1)}, f32[8,1024]{1,0:T(8,128)S(1)}) custom-call(bf16[384,4096]{1,0:T(8,128)(2,1)} %bitcast.28, bf16[4096,1024]{1,0:T(8,128)(2,1)} %gate_hbm.1, bf16[4096,1024]{1,0:T(8,128)(2,1)} %cand_hbm.1, f32[1,1024]{1,0:T(1,128)S(1)} %bitcast.20, ...), custom_call_target="tpu_custom_call" | custom-call | flops 6442450944 | bytes 16777216 | tf_op jit(solution)/shard_map/pallas_call | solution.py:277
  95.8 14.2 %all-gather = f32[64,1024]{1,0:T(8,128)S(1)} all-gather(f32[8,1024]{1,0:T(8,128)S(1)} %get-tuple-element.10), channel_id=2, replica_groups=mesh['seq'=8,'tp'=4] {'seq'}, dimensions={0}, use_global_device_ids=true | all-gather | bytes 294912 | tf_op jit(solution)/shard_map/all_gather | solution.py:299
  110.0 2.8 %shard_map.86.delta = bf16[2,384,1024]{2,1,0:T(8,128)(2,1)S(1)} custom-call(s32[1]{0:T(128)} %bitcast.where, f32[8,8,1024]{2,1,0:T(8,128)S(1)} %bitcast.17, f32[3,2,8,1024]{3,2,1,0:T(8,128)S(1)} %get-tuple-element.11.seg, f32[8,384,128]{2,1,0:T(8,128)S(1)} %get-tuple-element.12.keep, f32[8,384,128]{2,1,0:T(8,128)S(1)} %get-tuple-element.13.cand, ...), custom_call_target="tpu_custom_call" | custom-call | tf_op jit(solution)/shard_map/pallas_call | solution.py:301
  112.8 0.0 copy-start
  112.8 1.1 copy-done
  114.0 11.6 %all-gather.6.cloned.1.call-done = bf16[4,768,512]{2,1,0:T(8,128)(2,1)} async-done(((bf16[1,768,512]{2,1,0:T(8,128)(2,1)}), bf16[4,768,512]{2,1,0:T(8,128)(2,1)}) %all-gather.6.cloned.1.call-update) | async-done | bytes 3145744 | tf_op jit(solution)/shard_map/all_gather | solution.py:265
  125.6 3.9 %copy.19 = bf16[8,4,96,512]{3,2,1,0:T(8,128)(2,1)} copy(bf16[8,4,96,512]{3,2,0,1:T(8,128)(2,1)} %bitcast.21) | data formatting | bytes 6291456 | tf_op jit(solution)/shard_map/transpose | solution.py:267
  129.4 124.3 %shard_map.87 = (f32[512,1024]{1,0:T(8,128)}, f32[512,1024]{1,0:T(8,128)}, bf16[384,1024]{1,0:T(8,128)(2,1)}) custom-call(bf16[2,384,1024]{2,1,0:T(8,128)(2,1)} %copy-done, bf16[8,384,512]{2,1,0:T(8,128)(2,1)} %bitcast.22, bf16[4096,1024]{1,0:T(8,128)(2,1)} %gate_hbm.1, bf16[4096,1024]{1,0:T(8,128)(2,1)} %cand_hbm.1), custom_call_target="tpu_custom_call" | custom-call | flops 19327352832 | bytes 25165824 | tf_op jit(solution)/shard_map/pallas_call | solution.py:324
  253.7 0.0 copy-start.3
  253.7 3.3 %copy.26 = f32[512,1024]{1,0:T(8,128)} copy(f32[512,1024]{1,0:T(8,128)} %get-tuple-element.20) | data formatting | bytes 4194304
  257.0 0.0 copy-done.3
  257.0 0.0 copy-start.4
  257.0 1.3 copy.27
  258.3 0.4 copy-done.4
  258.7 0.9 copy.28
  (1 shorter events, 0.0 us)
Async XLA Ops:
  7.2 49.4 %all-gather.4.cloned.1.call-start = ((), (), s32[]{:S(2)}) async-start(), calls=%async_computation.1 | async-start | bytes 3932160 | tf_op jit(solution)/shard_map/all_gather | solution.py:256
  7.9 117.7 %all-gather.6.cloned.1.call-start = ((), (), s32[]{:S(2)}) async-start(), calls=%async_computation.2 | async-start | bytes 3932160 | tf_op jit(solution)/shard_map/all_gather | solution.py:265
  57.7 25.8 %copy-start.5 = (s32[2,192]{1,0:T(2,128)S(1)}, s32[2,192]{1,0:T(2,128)}, u32[]{:S(2)}) copy-start(s32[2,192]{1,0:T(2,128)} %param.11) | copy-start | bytes 4612
  57.8 26.0 %copy-start.1 = (bf16[2,192,1024]{2,1,0:T(8,128)(2,1)S(1)}, bf16[2,192,1024]{2,1,0:T(8,128)(2,1)}, u32[]{:S(2)}) copy-start(bf16[2,192,1024]{2,1,0:T(8,128)(2,1)} %param.10) | copy-start | bytes 2359300
  57.8 26.0 %copy-start.2 = (f32[1024]{0:T(1024)S(1)}, f32[1024]{0:T(1024)}, u32[]{:S(2)}) copy-start(f32[1024]{0:T(1024)} %param.9) | copy-start | bytes 12292
  112.8 1.1 copy-start
  253.7 3.3 %copy-start.3 = (f32[512,1024]{1,0:T(8,128)S(1)}, f32[512,1024]{1,0:T(8,128)}, u32[]{:S(2)}) copy-start(f32[512,1024]{1,0:T(8,128)} %get-tuple-element.21) | copy-start | bytes 6291460
  257.0 1.7 copy-start.4
Sparse Core Ops, SparseCore 0:
  9.8 46.6 all-gather.3
  83.6 41.8 all-gather.5

commit v4 on v3

v4 whole, which is shorter than its diff:
```python
import functools

import jax
import jax.numpy as jnp
from jax import lax
from jax.experimental import pallas as pl
from jax.experimental.pallas import tpu as pltpu
from jax.sharding import PartitionSpec as P

SEGS = 8
LANE = 128


def front_kernel(devices, groups, tokens, gate_hbm, cand_hbm, bias, read, scale, delta_out, cols_out,
                 flat, weights, acc, keep, cand, score, dp, dc, seg, spans, cols,
                 w_sem, own_sem, tok_send, tok_recv, col_send, col_recv, span_send, span_recv):
    seq = lax.axis_index("seq")
    tp = lax.axis_index("tp")
    mesh_id = pl.DeviceIdType.MESH
    f32 = jnp.float32
    rows, block = tokens.shape
    count = rows // 2
    steps = count // SEGS
    lanes = keep.shape[0]
    part, deep = cols.shape[1:]
    per = devices // groups
    pack = 2 if lanes % 2 == 0 else 1

    barrier = pltpu.get_barrier_semaphore()
    for d in range(1, groups):
        pl.semaphore_signal(barrier, inc=1, device_id=(seq, lax.rem(tp + d, groups)), device_id_type=mesh_id)
    for d in range(1, devices):
        pl.semaphore_signal(barrier, inc=1, device_id=(lax.rem(seq + d, devices), tp), device_id_type=mesh_id)

    def fetch(p):
        at = pl.ds(pl.multiple_of(lax.rem(tp + p, groups) * block, 128), block)
        return [
            pltpu.make_async_copy(w.at[at, :], weights.at[k, p], w_sem.at[k, p])
            for k, w in enumerate((gate_hbm, cand_hbm))
        ]

    for p in range(groups):
        for copy in fetch(p):
            copy.start()
    own = pltpu.make_async_copy(tokens, flat.at[tp], own_sem.at[0])
    own.start()
    pl.semaphore_wait(barrier, groups - 1 + devices - 1)

    def tell(d):
        return pltpu.make_async_remote_copy(
            src_ref=tokens, dst_ref=flat.at[tp], send_sem=tok_send.at[d], recv_sem=tok_recv.at[tp],
            device_id=(seq, lax.rem(tp + d, groups)), device_id_type=mesh_id)

    def hear(source):
        return pltpu.make_async_remote_copy(
            src_ref=tokens, dst_ref=flat.at[source], send_sem=tok_send.at[0], recv_sem=tok_recv.at[source],
            device_id=(seq, lax.rem(tp + 1, groups)), device_id_type=mesh_id)

    for d in range(1, groups):
        tell(d).start()
    own.wait()

    def piece(source, r):
        return flat.at[source, pl.ds(pl.multiple_of(tp * part, 16), part), r * deep : (r + 1) * deep]

    def scatter(source, r):
        target = source * per + r
        return pltpu.make_async_remote_copy(
            src_ref=piece(source, r), dst_ref=cols.at[seq], send_sem=col_send.at[target],
            recv_sem=col_recv.at[seq], device_id=(target, tp), device_id_type=mesh_id)

    def gather(source):
        return pltpu.make_async_remote_copy(
            src_ref=cols.at[seq], dst_ref=cols.at[source], send_sem=col_send.at[source],
            recv_sem=col_recv.at[source], device_id=(lax.rem(seq + 1, devices), tp), device_id_type=mesh_id)

    def keep_piece(source, r):
        return pltpu.make_async_copy(piece(source, r), cols.at[seq], own_sem.at[1])

    for p in range(groups):
        source = lax.rem(tp + groups - p, groups)
        if p > 0:
            hear(source).wait_recv()
        for r in range(per):

            @pl.when(source * per + r != seq)
            def _():
                scatter(source, r).start()

            @pl.when(source * per + r == seq)
            def _():
                keep_piece(source, r).start()

        slot = (groups - p) % groups
        for k, copy in enumerate(fetch(slot)):
            copy.wait()
            term = jnp.dot(flat[source], weights[k, slot], preferred_element_type=f32)
            acc[k] = term if p == 0 else acc[k] + term

    def lane_of(l):
        return pl.ds(pl.multiple_of(l * LANE, LANE), LANE)

    def first(gi, carry):
        pairs = [(b, gi * pack + i) for b in range(2) for i in range(pack)]
        for i in range(pack):
            l = gi * pack + i
            at = lane_of(l)
            keep[l] = jax.nn.sigmoid(acc[0, :, at] + bias[:, at])
            cand[l] = acc[1, :, at]
            score[l] = scale[...] * read[:, at].astype(f32)
        zero = jnp.zeros((SEGS, LANE), f32)
        muls = [zero + 1.0 for _ in pairs]
        adds = [zero for _ in pairs]
        gs = [zero for _ in pairs]
        for i in range(steps):
            for p, (b, l) in enumerate(pairs):
                at = pl.ds(b * count + i, SEGS, stride=steps)
                k = keep[l, at, :]
                c = cand[l, at, :]
                muls[p] = muls[p] * k
                adds[p] = k * adds[p] + (1.0 - k) * c
                at = pl.ds(b * count + steps - 1 - i, SEGS, stride=steps)
                gs[p] = keep[l, at, :] * (score[l, at, :] + gs[p])
        for p, (b, l) in enumerate(pairs):
            mul, add, g = muls[p], adds[p], gs[p]
            seg[0, b, l] = mul
            seg[1, b, l] = add
            seg[2, b, l] = g
            m = mul[0:1]
            a = add[0:1]
            r = g[SEGS - 1 :]
            for j in range(1, SEGS):
                m = m * mul[j : j + 1]
                a = mul[j : j + 1] * a + add[j : j + 1]
                e = SEGS - 1 - j
                r = mul[e : e + 1] * r + g[e : e + 1]
            spans[seq, l, b : b + 1, :] = m
            spans[seq, l, 2 + b : 3 + b, :] = a
            spans[seq, l, 4 + b : 5 + b, :] = r
        for i in range(pack):
            spans[seq, gi * pack + i, 6:8, :] = jnp.zeros((2, LANE), f32)
        return carry

    lax.fori_loop(0, lanes // pack, first, 0)

    def span(d):
        return pltpu.make_async_remote_copy(
            src_ref=spans.at[seq], dst_ref=spans.at[seq], send_sem=span_send.at[d], recv_sem=span_recv.at[seq],
            device_id=(lax.rem(seq + d, devices), tp), device_id_type=mesh_id)

    def span_from(d):
        source = lax.rem(seq + d, devices)
        return pltpu.make_async_remote_copy(
            src_ref=spans.at[source], dst_ref=spans.at[source], send_sem=span_send.at[d],
            recv_sem=span_recv.at[source], device_id=(source, tp), device_id_type=mesh_id)

    for d in range(1, devices):
        span(d).start()
    for d in range(1, devices):
        span_from(d).wait_recv()

    def second(gi, carry):
        pairs = [(b, gi * pack + i) for b in range(2) for i in range(pack)]
        states, tails = [], []
        for b, l in pairs:
            a = jnp.zeros((1, LANE), f32)
            r = a
            for d in range(devices):
                e = devices - 1 - d
                a = jnp.where(d < seq, spans[d, l, b : b + 1, :] * a + spans[d, l, 2 + b : 3 + b, :], a)
                r = jnp.where(e > seq, spans[e, l, b : b + 1, :] * r + spans[e, l, 4 + b : 5 + b, :], r)
            mul, add, g = seg[0, b, l], seg[1, b, l], seg[2, b, l]
            starts, ends = [a], [r]
            for j in range(SEGS - 1):
                a = mul[j : j + 1] * a + add[j : j + 1]
                starts.append(a)
                e = SEGS - 1 - j
                r = mul[e : e + 1] * r + g[e : e + 1]
                ends.append(r)
            states.append(jnp.concatenate(starts, axis=0))
            tails.append(jnp.concatenate(ends[::-1], axis=0))
        for i in range(steps):
            for p, (b, l) in enumerate(pairs):
                at = pl.ds(b * count + i, SEGS, stride=steps)
                k = keep[l, at, :]
                c = cand[l, at, :]
                dp[l, at, :] = (states[p] - c) * k * (1.0 - k)
                states[p] = k * states[p] + (1.0 - k) * c
        for i in range(steps):
            for p, (b, l) in enumerate(pairs):
                at = pl.ds(b * count + steps - 1 - i, SEGS, stride=steps)
                k = keep[l, at, :]
                adj = score[l, at, :] + tails[p]
                dp[l, at, :] = adj * dp[l, at, :]
                dc[l, at, :] = adj * (1.0 - k)
                tails[p] = k * adj
        for i in range(pack):
            l = gi * pack + i
            delta_out[0, :, lane_of(l)] = dp[l].astype(jnp.bfloat16)
            delta_out[1, :, lane_of(l)] = dc[l].astype(jnp.bfloat16)
        return carry

    lax.fori_loop(0, lanes // pack, second, 0)

    for d in range(1, groups):
        tell(d).wait_send()
    for d in range(1, devices):
        span(d).wait_send()
    for p in range(groups):
        source = lax.rem(tp + groups - p, groups)
        for r in range(per):

            @pl.when(source * per + r != seq)
            def _():
                scatter(source, r).wait_send()

            @pl.when(source * per + r == seq)
            def _():
                keep_piece(source, r).wait()

    for d in range(1, devices):
        gather(lax.rem(seq + d, devices)).wait_recv()
    cols_out[...] = cols[...]


def exchange_kernel(chips, groups, delta, mine_cols, gate_hbm, cand_hbm, gate_out, cand_out, tok_out,
                    slots, cols, weights, partial, landed, w_sem, own_sem, pass_sem, recv_sem, part_send, part_recv, col_send, col_recv):
    seq = lax.axis_index("seq")
    tp = lax.axis_index("tp")
    chip = lax.div(seq, 2)
    core = lax.rem(seq, 2)
    sibling = chip * 2 + 1 - core
    block = weights.shape[2]
    mesh_id = pl.DeviceIdType.MESH

    last = chips - 1
    right = jnp.minimum(chip + 1, last) * 2 + core
    left = jnp.maximum(chip - 1, 0) * 2 + core
    barrier = pltpu.get_barrier_semaphore()

    @pl.when(chip < last)
    def _():
        pl.semaphore_signal(barrier, inc=1, device_id=(right, tp), device_id_type=mesh_id)

    @pl.when(chip > 0)
    def _():
        pl.semaphore_signal(barrier, inc=1, device_id=(left, tp), device_id_type=mesh_id)

    pl.semaphore_signal(barrier, inc=1, device_id=(sibling, tp), device_id_type=mesh_id)
    for d in range(1, groups):
        pl.semaphore_signal(barrier, inc=1, device_id=(seq, lax.rem(tp + d, groups)), device_id_type=mesh_id)

    def fetch(p, buf):
        rows = pl.ds(pl.multiple_of(lax.rem(tp + p, groups) * block, 128), block)
        return [
            pltpu.make_async_copy(w.at[rows, :], weights.at[buf, k], w_sem.at[buf, k])
            for k, w in enumerate((gate_hbm, cand_hbm))
        ]

    for copy in fetch(1 % groups, 0):
        copy.start()
    pl.semaphore_wait(barrier, groups + jnp.minimum(chip, 1) + jnp.minimum(last - chip, 1))

    def pass_on(kind, origin, target, way):
        return pltpu.make_async_remote_copy(
            src_ref=slots.at[origin, kind], dst_ref=slots.at[origin, kind], send_sem=pass_sem.at[way, origin, kind],
            recv_sem=recv_sem.at[origin, kind], device_id=(target, tp), device_id_type=mesh_id)

    def own(kind):
        return pltpu.make_async_copy(delta.at[kind], slots.at[seq, kind], own_sem.at[kind])

    for kind in range(2):
        own(kind).start()
    for kind in range(2):
        own(kind).wait()

        @pl.when(chip < last)
        def _():
            pass_on(kind, seq, right, 0).start()

        @pl.when(chip > 0)
        def _():
            pass_on(kind, seq, left, 1).start()

        pass_on(kind, seq, sibling, 2).start()

    def spread(d):
        return pltpu.make_async_remote_copy(
            src_ref=mine_cols, dst_ref=cols.at[tp], send_sem=col_send.at[d], recv_sem=col_recv.at[tp],
            device_id=(seq, lax.rem(tp + d, groups)), device_id_type=mesh_id)

    def spread_from(d):
        source = lax.rem(tp + d, groups)
        return pltpu.make_async_remote_copy(
            src_ref=mine_cols, dst_ref=cols.at[source], send_sem=col_send.at[d], recv_sem=col_recv.at[source],
            device_id=(seq, source), device_id_type=mesh_id)

    own_cols = pltpu.make_async_copy(mine_cols, cols.at[tp], own_sem.at[2])
    own_cols.start()
    for d in range(1, groups):
        spread(d).start()

    nt = (((1,), (1,)), ((), ()))
    tn = (((0,), (0,)), ((), ()))
    f32 = jnp.float32

    def share(p, buf):
        for copy in fetch(p, buf):
            copy.wait()
        term = lax.dot_general(delta[0], weights[buf, 0], nt, preferred_element_type=f32)
        return term + lax.dot_general(delta[1], weights[buf, 1], nt, preferred_element_type=f32)

    def give(p):
        return pltpu.make_async_remote_copy(
            src_ref=partial.at[p - 1], dst_ref=landed.at[p - 1], send_sem=part_send.at[p - 1],
            recv_sem=part_recv.at[p - 1], device_id=(seq, lax.rem(tp + p, groups)), device_id_type=mesh_id)

    for p in range(1, groups):
        for copy in fetch((p + 1) % groups, p % 2):
            copy.start()
        partial[p - 1] = share(p, (p - 1) % 2).astype(jnp.bfloat16)
        give(p).start()
    mine = share(0, (groups - 1) % 2)
    for p in range(1, groups):
        give(p).wait()
        mine = mine + landed[p - 1].astype(f32)
    tok_out[...] = mine.astype(jnp.bfloat16)

    own_cols.wait()
    for d in range(1, groups):
        spread(d).wait_send()
        spread_from(d).wait_recv()
    gate_out[...] = jnp.zeros_like(gate_out)
    cand_out[...] = jnp.zeros_like(cand_out)
    for kind, out in enumerate((gate_out, cand_out)):

        def take(origin):
            rows = jnp.concatenate([cols[g, origin] for g in range(groups)], axis=0)
            out[...] += lax.dot_general(rows, slots[origin, kind], tn, preferred_element_type=f32)

        take(seq)
        pass_on(kind, sibling, sibling, 2).wait_recv()
        take(sibling)

        def step(e, carry):
            dist = lax.div(e, 2) + 1
            from_left = lax.rem(e, 2) == 0
            origin_chip = jnp.where(from_left, chip - dist, chip + dist)

            @pl.when((origin_chip >= 0) & (origin_chip <= last))
            def _():
                origin = origin_chip * 2 + core
                pass_on(kind, origin, sibling, 2).wait_recv()

                @pl.when(from_left & (chip < last))
                def _():
                    pass_on(kind, origin, right, 0).start()

                @pl.when(jnp.logical_not(from_left) & (chip > 0))
                def _():
                    pass_on(kind, origin, left, 1).start()

                pass_on(kind, origin, sibling, 2).start()
                take(origin)
                other = origin_chip * 2 + 1 - core
                pass_on(kind, other, sibling, 2).wait_recv()
                take(other)

            return carry

        lax.fori_loop(0, 2 * last, step, 0)
    for kind in range(2):

        def drain(o, carry):
            origin = o * 2 + core

            @pl.when((o <= chip) & (chip < last))
            def _():
                pass_on(kind, origin, right, 0).wait_send()

            @pl.when((o >= chip) & (chip > 0))
            def _():
                pass_on(kind, origin, left, 1).wait_send()

            pass_on(kind, origin, sibling, 2).wait_send()
            return carry

        lax.fori_loop(0, chips, drain, 0)


def shards(tokens, gate_weight, cand_weight, forget_bias, readout, advantage):
    devices = lax.axis_size("seq")
    groups = lax.axis_size("tp")
    count = tokens.shape[1]
    rows = 2 * count
    depth, width = gate_weight.shape
    block = depth // groups
    part = rows // groups
    deep = depth // devices
    lanes = width // LANE
    f32 = jnp.float32
    bf16 = jnp.bfloat16
    dma = pltpu.SemaphoreType.DMA
    vmem = pl.BlockSpec(memory_space=pltpu.VMEM)
    hbm = pl.BlockSpec(memory_space=pl.ANY)
    scale = (advantage.astype(f32) * 0.25).reshape(rows, 1)
    plane = pltpu.VMEM((lanes, rows, LANE), f32)
    delta, cols = pl.pallas_call(
        functools.partial(front_kernel, devices, groups),
        in_specs=[vmem, hbm, hbm, vmem, vmem, vmem],
        out_specs=[vmem, vmem],
        out_shape=[
            jax.ShapeDtypeStruct((2, rows, width), bf16),
            jax.ShapeDtypeStruct((devices, part, deep), bf16),
        ],
        scratch_shapes=[
            pltpu.VMEM((groups, rows, block), bf16),
            pltpu.VMEM((2, groups, block, width), bf16),
            pltpu.VMEM((2, rows, width), f32),
            plane,
            plane,
            plane,
            plane,
            plane,
            pltpu.VMEM((3, 2, lanes, SEGS, LANE), f32),
            pltpu.VMEM((devices, lanes, 8, LANE), f32),
            pltpu.VMEM((devices, part, deep), bf16),
            dma((2, groups)),
            dma((2,)),
            dma((groups,)),
            dma((groups,)),
            dma((devices,)),
            dma((devices,)),
            dma((devices,)),
            dma((devices,)),
        ],
        compiler_params=pltpu.CompilerParams(collective_id=2, has_side_effects=True, vmem_limit_bytes=56 << 20),
        cost_estimate=pl.CostEstimate(flops=4 * rows * depth * width, bytes_accessed=20 << 20, transcendentals=rows * width),
    )(tokens.reshape(rows, block), gate_weight, cand_weight, forget_bias.reshape(1, width), readout.reshape(rows, width), scale)

    chips = devices // 2
    grad_gate, grad_cand, grad_tokens = pl.pallas_call(
        functools.partial(exchange_kernel, chips, groups),
        in_specs=[vmem, vmem, hbm, hbm],
        out_specs=[vmem, vmem, vmem],
        out_shape=[
            jax.ShapeDtypeStruct((depth // devices, width), f32),
            jax.ShapeDtypeStruct((depth // devices, width), f32),
            jax.ShapeDtypeStruct((rows, block), bf16),
        ],
        scratch_shapes=[
            pltpu.VMEM((devices, 2, rows, width), bf16),
            pltpu.VMEM((groups, devices, part, deep), bf16),
            pltpu.VMEM((2, 2, block, width), bf16),
            pltpu.VMEM((groups - 1, rows, block), bf16),
            pltpu.VMEM((groups - 1, rows, block), bf16),
            dma((2, 2)),
            dma((3,)),
            dma((3, devices, 2)),
            dma((devices, 2)),
            dma((groups - 1,)),
            dma((groups - 1,)),
            dma((groups,)),
            dma((groups,)),
        ],
        compiler_params=pltpu.CompilerParams(collective_id=1, has_side_effects=True, vmem_limit_bytes=56 << 20),
        cost_estimate=pl.CostEstimate(flops=12 * rows * depth * width, bytes_accessed=24 << 20, transcendentals=0),
    )(delta, cols, gate_weight, cand_weight)
    return (grad_gate, grad_cand, grad_tokens.reshape(2, count, block))


def solution(mesh):
    in_specs = (
        P(None, "seq", "tp"),
        P(None, "tp"),
        P(None, "tp"),
        P("tp"),
        P(None, "seq", "tp"),
        P(None, "seq"),
    )
    out_specs = (P("seq", "tp"), P("seq", "tp"), P(None, "seq", "tp"))
    return jax.shard_map(shards, mesh=mesh, in_specs=in_specs, out_specs=out_specs, check_vma=False)
```

time: 267 us -> 226 us (0.85)
  Pallas kernels: 139 us -> 216 us
  waiting for transfers between devices: 60.9 us -> 0 us
  blocking collectives: 39.8 us -> 0 us
  between operations: 14.2 us -> 0.66 us
  local copies, waits for them, and re-layouts: 12.3 us -> 6.75 us
    all_gather x2 -> x0, waiting for transfers between devices: 60.2 us -> none  [the longest x1 48.6 us: shards(): whole = lax.all_gather(tokens, 'tp', axis=2, tiled=True)]
    pallas_call x2 -> x1, Pallas kernels: 14.9 us -> 62.9 us  [shards(): pl.pallas_call(functools.partial(front_kernel, devices, groups), in_specs...]
    pallas_call x1, Pallas kernels: 124 us -> 153 us  [shards(): pl.pallas_call(functools.partial(exchange_kernel, chips, groups), in_spec...]
    all_to_all x1 -> x0, blocking collectives: 25.6 us -> none  [shards(): mine = lax.all_to_all(mine, 'seq', split_axis=1, concat_axis=0, tiled=True)]
    all_gather x1 -> x0, blocking collectives: 14.2 us -> none  [shards(): spans = lax.all_gather(span, 'seq', axis=0, tiled=False)]
    transpose x1 -> x0, local copies, waits for them, and re-layouts: 3.85 us -> none  [shards(): jnp.transpose(cols, (1, 0, 2, 3)).reshape(devices, rows, depth // devices)]
    unnamed x15 -> x7, local copies, waits for them, and re-layouts: 7.02 us -> 5.87 us
  transfers between devices with their start and end apart: 2 -> 0, of which waited for: 2 -> 0; matrix products, arithmetic and copies ran while one was open for 0% -> 0% of each run, Pallas kernels for 6% -> 0%
where the time goes in v4:
time: 226 us; the launch traced here: 224 us
  Pallas kernels  216 us (96%)
  local copies, waits for them, and re-layouts  6.75 us (3%)
    pallas_call x1, Pallas kernels, shards(): pl.pallas_call(functools.partial(exchange_kernel, chips, groups), in_spec...  153 us
    pallas_call x1, Pallas kernels, shards(): pl.pallas_call(functools.partial(front_kernel, devices, groups), in_specs...  62.9 us
    unnamed x7, local copies, waits for them, and re-layouts  5.87 us

profile of v4, /device:TPU:0, one launch (start us, length us, event | category | flops | bytes accessed | tf_op | source)
XLA Modules:
  0.0 224.0 jit_solution(804061972887419732)
XLA Ops:
  0.6 0.7 convert_multiply_fusion
  1.3 0.9 reshape.26.scale
  2.2 62.9 %shard_map.85 = (bf16[2,384,1024]{2,1,0:T(8,128)(2,1)}, bf16[8,96,512]{2,1,0:T(8,128)(2,1)}) custom-call(bf16[384,1024]{1,0:T(8,128)(2,1)} %bitcast.5, bf16[4096,1024]{1,0:T(8,128)(2,1)} %gate_hbm.3, bf16[4096,1024]{1,0:T(8,128)(2,1)} %cand_hbm.3, f32[1,1024]{1,0:T(1,128)} %bitcast.7, bf16[384,1024]{1,0:T(8,128)(2,1)} %bitcast.6, f32[384,1]{1,0:T(8,128)} %reshape.26.scale), custom_call_target="tpu_custom_call" | custom-call | flops 6442450944 | bytes 20971520 | tf_op jit(solution)/shard_map/pallas_call | solution.py:408
  65.1 153.1 %shard_map.86 = (f32[512,1024]{1,0:T(8,128)}, f32[512,1024]{1,0:T(8,128)}, bf16[384,1024]{1,0:T(8,128)(2,1)}) custom-call(bf16[2,384,1024]{2,1,0:T(8,128)(2,1)} %get-tuple-element.8.delta, bf16[8,96,512]{2,1,0:T(8,128)(2,1)} %get-tuple-element.9.mine_cols, bf16[4096,1024]{1,0:T(8,128)(2,1)} %gate_hbm.3, bf16[4096,1024]{1,0:T(8,128)(2,1)} %cand_hbm.3), custom_call_target="tpu_custom_call" | custom-call | flops 19327352832 | bytes 25165824 | tf_op jit(solution)/shard_map/pallas_call | solution.py:442
  218.2 0.0 copy-start
  218.2 3.3 %copy.13 = f32[512,1024]{1,0:T(8,128)} copy(f32[512,1024]{1,0:T(8,128)} %get-tuple-element.16) | data formatting | bytes 4194304
  221.5 0.0 copy-done
  221.5 0.0 copy-start.1
  221.5 1.3 copy.14
  222.8 0.4 copy-done.1
  223.2 0.9 copy.15
Async XLA Ops:
  218.2 3.3 %copy-start = (f32[512,1024]{1,0:T(8,128)S(1)}, f32[512,1024]{1,0:T(8,128)}, u32[]{:S(2)}) copy-start(f32[512,1024]{1,0:T(8,128)} %get-tuple-element.17) | copy-start | bytes 6291460
  221.5 1.7 copy-start.1
